TPU v7x, 256 devices: a whole 4x4x8 slice. The times are simulated.
256 devices in a mesh: shot: 8 (over x, y_hi), sub: 32 (over y_lo, z, core).
Axes of the slice: x: 4, y: 4 (y_hi: 2, y_lo: 2; y = y_hi * 2 + y_lo), z: 8, core: 2. Of those that a mesh axis runs over, the one named last changes fastest.
Arguments:
- vel_model: bfloat16 [8, 128, 320, 128], P('shot', 'sub'), may hold values from 0.5 to 1
- den_model: bfloat16 [8, 128, 320, 128], P('shot', 'sub'), may hold values from 1 to 4
- cover: int32 [8, 32], replicated, may hold values from 0 to 7
- receivers: int32 [8, 512], P('shot'), may hold values from 0 to 5242879
- observed: float32 [8, 4, 512], P('shot'), may hold values from -6 to 6
- p_now: float32 [8, 128, 320, 128], P('shot', 'sub'), may hold values from -6 to 6
- p_before: float32 [8, 128, 320, 128], P('shot', 'sub'), may hold values from -6 to 6
- q_now: float32 [8, 128, 320, 128], P('shot', 'sub'), may hold values from -6 to 6
- q_before: float32 [8, 128, 320, 128], P('shot', 'sub'), may hold values from -6 to 6
Outputs:
- grad_vel: float32 [8, 128, 320, 128], P('shot', 'sub')
- grad_den: float32 [8, 128, 320, 128], P('shot', 'sub')
All inputs are finite; a program needn't handle non-finite values.
Results may differ from a plain program's by a relative error of at most 0.011.
Values may be sent and summed in bfloat16 or wider, within the bound.
A program may use at most 64 MiB of HBM per device.

v0:
```python
import jax
import jax.numpy as jnp
from jax import lax
from jax.sharding import PartitionSpec as P

ITERS = 4


SECOND = (-205.0 / 72.0, 8.0 / 5.0, -1.0 / 5.0, 8.0 / 315.0, -1.0 / 560.0)
FIRST = (4.0 / 5.0, -1.0 / 5.0, 4.0 / 105.0, -1.0 / 280.0)
SPEED = 0.15


def padded_2(cells, sides, width):
    for axis, dim in sides:
        count = lax.axis_size(axis)
        ends = count - 1
        head = lax.slice_in_dim(cells, 0, width, axis=dim)
        tail = lax.slice_in_dim(cells, cells.shape[dim] - width, cells.shape[dim], axis=dim)
        cells = jnp.concatenate(
            [
                lax.ppermute(tail, axis, [(i, (i + 1) % count) for i in range(ends)]),
                cells,
                lax.ppermute(head, axis, [((i + 1) % count, i) for i in range(ends)]),
            ],
            axis=dim,
        )
    return cells


def moved(padded, direction, offset):
    window = [
        slice(4, padded.shape[0] - 4),
        slice(4, padded.shape[1] - 4),
        slice(4, padded.shape[2] - 4),
    ]
    window[direction] = slice(4 + offset, padded.shape[direction] - 4 + offset)
    return padded[tuple(window)]


def stencil(padded):
    center = moved(padded, 0, 0)
    laplace = 3.0 * SECOND[0] * center
    first_diffs = []
    for direction in range(3):
        slope_sum = jnp.zeros_like(center)
        for distance in range(1, 5):
            above_part = moved(padded, direction, distance)
            below_part = moved(padded, direction, -distance)
            laplace = laplace + SECOND[distance] * (above_part + below_part)
            slope_sum = slope_sum + FIRST[distance - 1] * (above_part - below_part)
        first_diffs.append(slope_sum)
    return (laplace, first_diffs)


def operate(laplace, first_diffs, slopes):
    return laplace - (
        slopes[0] * first_diffs[0] + slopes[1] * first_diffs[1] + slopes[2] * first_diffs[2]
    )


def side_pad(wide):
    return jnp.pad(wide, ((0, 0), (4, 4), (4, 4)))


def body(vel_model, den_model, cover, receivers, observed, p_now, p_before, q_now, q_before):
    shot_index = lax.axis_index("shot")
    column = lax.axis_index("sub")
    groups = lax.axis_size("shot")
    wanted = cover[shot_index, column]
    pieces = (
        lax.all_gather(vel_model, "shot", axis=0, tiled=True),
        lax.all_gather(den_model, "shot", axis=0, tiled=True),
    )
    rows = jnp.arange(pieces[0].shape[0], dtype=jnp.int32)
    chosen = (rows == wanted)[:, None, None, None]
    vel_part = jnp.sum(jnp.where(chosen, pieces[0], jnp.zeros_like(pieces[0])), axis=0)
    den_part = jnp.sum(jnp.where(chosen, pieces[1], jnp.zeros_like(pieces[1])), axis=0)
    velocity = vel_part.astype(jnp.float32)
    density = den_part.astype(jnp.float32)
    log_den = jnp.log(density)
    wide_log = padded_2(log_den.astype(jnp.bfloat16), (("sub", 0),), 4).astype(log_den.dtype)
    unused_lap, slopes = stencil(side_pad(wide_log))
    scale = SPEED * velocity * velocity
    shape = velocity.shape
    cells = velocity.size
    local_cell = receivers[0] - column * cells
    valid = (local_cell >= 0) & (local_cell < cells)
    station = jnp.where(valid, local_cell, 0)

    def field_terms(field):
        wide = padded_2(field.astype(jnp.bfloat16), (("sub", 0),), 4).astype(field.dtype)
        laplace, diffs = stencil(side_pad(wide))
        return (operate(laplace, diffs, slopes), diffs)

    stored = []
    misfits = []
    previous, current = (p_before[0], p_now[0])
    for time_step in range(ITERS):
        applied, diffs = field_terms(current)
        stored.append((applied, diffs))
        previous, current = (current, 2.0 * current - previous + scale * applied)
        sampled = current.reshape(-1)[station]
        misfits.append(jnp.where(valid, sampled - observed[0, time_step], 0.0))
    sum_vel = jnp.zeros(shape, jnp.float32)
    sum_den = jnp.zeros(shape, jnp.float32)
    previous, current = (q_before[0], q_now[0])
    for time_step in range(ITERS):
        source = (
            jnp.zeros((cells,), jnp.float32)
            .at[station]
            .add(misfits[ITERS - 1 - time_step])
            .reshape(shape)
        )
        adjoint = current + source
        applied, diffs = field_terms(adjoint)
        forward_applied, forward_diffs = stored[ITERS - 1 - time_step]
        sum_vel = sum_vel + adjoint * forward_applied
        sum_den = sum_den + (
            diffs[0] * forward_diffs[0] + diffs[1] * forward_diffs[1] + diffs[2] * forward_diffs[2]
        )
        previous, current = (current, 2.0 * adjoint - previous + scale * applied)
    shot_vel = (2.0 * SPEED * velocity * sum_vel).astype(jnp.bfloat16)
    shot_den = (scale / density * sum_den).astype(jnp.bfloat16)
    targets = (jnp.arange(groups, dtype=jnp.int32) == wanted)[:, None, None, None]
    exact_vel = lax.optimization_barrier(shot_vel).astype(jnp.float32)
    exact_den = lax.optimization_barrier(shot_den).astype(jnp.float32)
    term_vel = jnp.where(targets, exact_vel[None], 0.0)
    term_den = jnp.where(targets, exact_den[None], 0.0)
    summed_vel, summed_den = (
        lax.psum_scatter(
            term_vel.astype(jnp.bfloat16), "shot", scatter_dimension=0, tiled=True
        ).astype(jnp.float32),
        lax.psum_scatter(
            term_den.astype(jnp.bfloat16), "shot", scatter_dimension=0, tiled=True
        ).astype(jnp.float32),
    )
    return (summed_vel, summed_den)


def solution(mesh):
    return jax.shard_map(
        body,
        mesh=mesh,
        in_specs=(
            P("shot", "sub", None, None),
            P("shot", "sub", None, None),
            P(),
            P("shot", None),
            P("shot", None, None),
            P("shot", "sub", None, None),
            P("shot", "sub", None, None),
            P("shot", "sub", None, None),
            P("shot", "sub", None, None),
        ),
        out_specs=(P("shot", "sub", None, None), P("shot", "sub", None, None)),
        check_vma=False,
    )
```

profile of v0, /device:TPU:232, one launch (start us, length us, event | category | flops | bytes accessed | tf_op | source)
XLA Modules:
  0.0 528.0 jit_solution(1887981867650907972)
XLA Ops:
  16.1 57.9 %all-gather.3.cloned.1.call-done = bf16[8,4,320,128]{3,2,1,0:T(8,128)(2,1)} async-done(((bf16[1,4,320,128]{3,2,1,0:T(8,128)(2,1)}), bf16[8,4,320,128]{3,2,1,0:T(8,128)(2,1)}) %all-gather.3.cloned.1.call-update) | async-done | bytes 2621456 | tf_op jit(solution)/shard_map/all_gather | solution.py:72
  74.0 65.4 %all-gather.5.cloned.1.call-done = bf16[8,4,320,128]{3,2,1,0:T(8,128)(2,1)} async-done(((bf16[1,4,320,128]{3,2,1,0:T(8,128)(2,1)}), bf16[8,4,320,128]{3,2,1,0:T(8,128)(2,1)}) %all-gather.5.cloned.1.call-update) | async-done | bytes 2621456 | tf_op jit(solution)/shard_map/all_gather | solution.py:73
  139.4 3.6 select_reduce_fusion
  149.8 3.8 collective-permute-done.2
  153.8 6.6 %fusion.197 = (bf16[4,320,128]{2,1,0:T(8,128)(2,1)}, f32[4,320,128]{2,1,0:T(8,128)}, f32[4,320,128]{2,1,0:T(8,128)}, f32[4,320,128]{2,1,0:T(8,128)}, f32[4,320,1...) fusion(bf16[4,320,128]{2,1,0:T(8,128)(2,1)S(1)} %get-tuple-elem, ...), kind=kLoop, calls=%fused_computation.411 | loop fusion | flops 19169280 | bytes 22282240 | tf_op jit(solution)/shard_map/convert_element_type | solution.py:92
  167.4 3.8 collective-permute-done.4
  172.5 3.9 fusion.194
  182.9 3.8 collective-permute-done.6
  186.9 4.2 fusion.191
  193.0 3.3 collective-permute-start.8
  199.5 20.5 %gather_fusion.2 = f32[512]{0:T(512)S(1)} fusion(f32[163840]{0:T(1024)} %bitcast.50, s32[1024]{0:T(1024)S(1)} %pad_clamp_fusion), kind=kCustom, calls=%fused_computation.2 | custom fusion | bytes 6144 | tf_op jit(solution)/shard_map/gather | solution.py:103
  220.0 20.5 %gather_fusion.1 = f32[512]{0:T(512)S(1)} fusion(f32[163840]{0:T(1024)} %bitcast.51, s32[1024]{0:T(1024)S(1)} %pad_clamp_fusion), kind=kCustom, calls=%fused_computation.1 | custom fusion | bytes 6144 | tf_op jit(solution)/shard_map/gather | solution.py:103
  242.0 4.1 fusion.10
  246.0 20.5 %gather_fusion = f32[512]{0:T(512)S(1)} fusion(f32[163840]{0:T(1024)} %bitcast.52, s32[1024]{0:T(1024)S(1)} %pad_clamp_fusion), kind=kCustom, calls=%fused_computation | custom fusion | bytes 6144 | tf_op jit(solution)/shard_map/gather | solution.py:103
  266.5 4.2 scatter_custom_fusion
  277.6 4.9 scatter_custom_fusion.1
  285.7 4.0 add_convert_fusion
  294.8 4.9 scatter_custom_fusion.2
  302.5 4.0 fusion.187
  311.8 4.9 scatter_custom_fusion.3
  329.7 5.5 %collective-permute-done.16 = bf16[4,320,128]{2,1,0:T(8,128)(2,1)S(1)} collective-permute-done((bf16[4,320,128]{2,1,0:T(8,128)(2,1)S(1)}, bf16[4,320,128]{2,1,0:T(8,128)(2,1)S(1)}, u32[]{:S(2)}, u32[]{:S(2)}) %collective-permute-start.16) | collective-permute-done | bytes 327712 | tf_op jit(solution)/shard_map/ppermute | solution.py:22
  338.3 3.7 select_convert_fusion
  342.6 90.6 %reduce-scatter.3.cloned.1.call-done = bf16[1,4,320,128]{3,2,1,0:T(8,128)(2,1)} async-done(((bf16[8,4,320,128]{3,2,1,0:T(8,128)(2,1)}), bf16[1,4,320,128]{3,2,1,0:T(8,128)(2,1)}) %reduce-scatter.3.cloned.1.call-update) | async-done | bytes 327696 | tf_op jit(solution)/shard_map/reduce_scatter | solution.py:131
  435.1 84.5 %reduce-scatter.5.cloned.1.call-done = bf16[1,4,320,128]{3,2,1,0:T(8,128)(2,1)} async-done(((bf16[8,4,320,128]{3,2,1,0:T(8,128)(2,1)}), bf16[1,4,320,128]{3,2,1,0:T(8,128)(2,1)}) %reduce-scatter.5.cloned.1.call-update) | async-done | bytes 327696 | tf_op jit(solution)/shard_map/reduce_scatter | solution.py:134
  (146 shorter events, 80.2 us)
Async XLA Ops:
  7.2 66.8 %all-gather.3.cloned.1.call-start = ((), (), s32[]{:S(2)}) async-start(), calls=%async_computation.2 | async-start | bytes 2949120 | tf_op jit(solution)/shard_map/all_gather | solution.py:72
  7.9 131.5 %all-gather.5.cloned.1.call-start = ((), (), s32[]{:S(2)}) async-start(), calls=%async_computation.3 | async-start | bytes 2949120 | tf_op jit(solution)/shard_map/all_gather | solution.py:73
  8.6 424.6 %reduce-scatter.3.cloned.1.call-start = ((), (), s32[]{:S(2)}) async-start(), calls=%async_computation.4 | async-start | bytes 2949120 | tf_op jit(solution)/shard_map/reduce_scatter | solution.py:131
  9.8 137.7 %collective-permute-start.1 = (bf16[4,320,128]{2,1,0:T(8,128)(2,1)S(1)}, bf16[4,320,128]{2,1,0:T(8,128)(2,1)S(1)}, u32[]{:S(2)}, u32[]{:S(2)}) collective-permute-start(bf16[4,320,128]{2,1,0:T(8,128)(2,1)S(1)} %bitcast_convert_fusion), channel_id=1, source_target_pairs={{1,0},{2,1},{3,2},{4,3},{5,4},{6,5},{7,6},{8,7},{9,8},{10,9},{11,1... | collective-permute-start | bytes 983048 | tf_op jit(solution)/shard_map/ppermute | solution.py:24
  12.2 135.4 %collective-permute-start = (bf16[4,320,128]{2,1,0:T(8,128)(2,1)S(1)}, bf16[4,320,128]{2,1,0:T(8,128)(2,1)S(1)}, u32[]{:S(2)}, u32[]{:S(2)}) collective-permute-start(bf16[4,320,128]{2,1,0:T(8,128)(2,1)S(1)} %bitcast_convert_fusion), channel_id=1, source_target_pairs={{0,1},{1,2},{2,3},{3,4},{4,5},{5,6},{6,7},{7,8},{8,9},{9,10},{10,1... | collective-permute-start | bytes 983048 | tf_op jit(solution)/shard_map/ppermute | solution.py:22
  143.2 6.7 %collective-permute-start.3 = (bf16[4,320,128]{2,1,0:T(8,128)(2,1)S(1)}, bf16[4,320,128]{2,1,0:T(8,128)(2,1)S(1)}, u32[]{:S(2)}, u32[]{:S(2)}) collective-permute-start(bf16[4,320,128]{2,1,0:T(8,128)(2,1)S(1)} %fusion.18), channel_id=1, source_target_pairs={{1,0},{2,1},{3,2},{4,3},{5,4},{6,5},{7,6},{8,7},{9,8},{10,9},{11,1... | collective-permute-start | bytes 983048 | tf_op jit(solution)/shard_map/ppermute | solution.py:24
  145.3 8.4 %collective-permute-start.2 = (bf16[4,320,128]{2,1,0:T(8,128)(2,1)S(1)}, bf16[4,320,128]{2,1,0:T(8,128)(2,1)S(1)}, u32[]{:S(2)}, u32[]{:S(2)}) collective-permute-start(bf16[4,320,128]{2,1,0:T(8,128)(2,1)S(1)} %fusion.18), channel_id=1, source_target_pairs={{0,1},{1,2},{2,3},{3,4},{4,5},{5,6},{6,7},{7,8},{8,9},{9,10},{10,1... | collective-permute-start | bytes 983048 | tf_op jit(solution)/shard_map/ppermute | solution.py:22
  160.4 6.9 %collective-permute-start.5 = (bf16[4,320,128]{2,1,0:T(8,128)(2,1)}, bf16[4,320,128]{2,1,0:T(8,128)(2,1)}, u32[]{:S(2)}, u32[]{:S(2)}) collective-permute-start(bf16[4,320,128]{2,1,0:T(8,128)(2,1)} %get-tuple-element.36), channel_id=1, source_target_pairs={{1,0},{2,1},{3,2},{4,3},{5,4},{6,5},{7,6},{8,7},{9,8},{10,9},{11,1... | collective-permute-start | bytes 983048 | tf_op jit(solution)/shard_map/ppermute | solution.py:24
  162.5 8.7 %collective-permute-start.4 = (bf16[4,320,128]{2,1,0:T(8,128)(2,1)}, bf16[4,320,128]{2,1,0:T(8,128)(2,1)}, u32[]{:S(2)}, u32[]{:S(2)}) collective-permute-start(bf16[4,320,128]{2,1,0:T(8,128)(2,1)} %get-tuple-element.36), channel_id=1, source_target_pairs={{0,1},{1,2},{2,3},{3,4},{4,5},{5,6},{6,7},{7,8},{8,9},{9,10},{10,1... | collective-permute-start | bytes 983048 | tf_op jit(solution)/shard_map/ppermute | solution.py:22
  176.4 6.5 %collective-permute-start.7 = (bf16[4,320,128]{2,1,0:T(8,128)(2,1)S(1)}, bf16[4,320,128]{2,1,0:T(8,128)(2,1)S(1)}, u32[]{:S(2)}, u32[]{:S(2)}) collective-permute-start(bf16[4,320,128]{2,1,0:T(8,128)(2,1)S(1)} %get-tuple-element.30), channel_id=1, source_target_pairs={{1,0},{2,1},{3,2},{4,3},{5,4},{6,5},{7,6},{8,7},{9,8},{10,9},{11,1... | collective-permute-start | bytes 983048 | tf_op jit(solution)/shard_map/ppermute | solution.py:24
  178.3 8.4 %collective-permute-start.6 = (bf16[4,320,128]{2,1,0:T(8,128)(2,1)S(1)}, bf16[4,320,128]{2,1,0:T(8,128)(2,1)S(1)}, u32[]{:S(2)}, u32[]{:S(2)}) collective-permute-start(bf16[4,320,128]{2,1,0:T(8,128)(2,1)S(1)} %get-tuple-element.30), channel_id=1, source_target_pairs={{0,1},{1,2},{2,3},{3,4},{4,5},{5,6},{6,7},{7,8},{8,9},{9,10},{10,1... | collective-permute-start | bytes 983048 | tf_op jit(solution)/shard_map/ppermute | solution.py:22
  191.1 49.5 %collective-permute-start.9 = (bf16[4,320,128]{2,1,0:T(8,128)(2,1)}, bf16[4,320,128]{2,1,0:T(8,128)(2,1)}, u32[]{:S(2)}, u32[]{:S(2)}) collective-permute-start(bf16[4,320,128]{2,1,0:T(8,128)(2,1)} %get-tuple-element.24), channel_id=1, source_target_pairs={{1,0},{2,1},{3,2},{4,3},{5,4},{6,5},{7,6},{8,7},{9,8},{10,9},{11,1... | collective-permute-start | bytes 983048 | tf_op jit(solution)/shard_map/ppermute | solution.py:24
  193.0 47.6 %collective-permute-start.8 = (bf16[4,320,128]{2,1,0:T(8,128)(2,1)}, bf16[4,320,128]{2,1,0:T(8,128)(2,1)}, u32[]{:S(2)}, u32[]{:S(2)}) collective-permute-start(bf16[4,320,128]{2,1,0:T(8,128)(2,1)} %get-tuple-element.24), channel_id=1, source_target_pairs={{0,1},{1,2},{2,3},{3,4},{4,5},{5,6},{6,7},{7,8},{8,9},{9,10},{10,1... | collective-permute-start | bytes 983048 | tf_op jit(solution)/shard_map/ppermute | solution.py:22
  220.0 21.9 %copy-start.2 = (f32[4,320,128]{2,1,0:T(8,128)S(1)}, f32[4,320,128]{2,1,0:T(8,128)}, u32[]{:S(2)}) copy-start(f32[4,320,128]{2,1,0:T(8,128)} %copy-done.1) | copy-start | bytes 1966084
  272.6 9.9 %collective-permute-start.11 = (bf16[4,320,128]{2,1,0:T(8,128)(2,1)}, bf16[4,320,128]{2,1,0:T(8,128)(2,1)}, u32[]{:S(2)}, u32[]{:S(2)}) collective-permute-start(bf16[4,320,128]{2,1,0:T(8,128)(2,1)} %fusion.184), channel_id=1, source_target_pairs={{1,0},{2,1},{3,2},{4,3},{5,4},{6,5},{7,6},{8,7},{9,8},{10,9},{11,1... | collective-permute-start | bytes 983048 | tf_op jit(solution)/shard_map/ppermute | solution.py:24
  275.7 8.7 %collective-permute-start.10 = (bf16[4,320,128]{2,1,0:T(8,128)(2,1)}, bf16[4,320,128]{2,1,0:T(8,128)(2,1)}, u32[]{:S(2)}, u32[]{:S(2)}) collective-permute-start(bf16[4,320,128]{2,1,0:T(8,128)(2,1)} %fusion.184), channel_id=1, source_target_pairs={{0,1},{1,2},{2,3},{3,4},{4,5},{5,6},{6,7},{7,8},{8,9},{9,10},{10,1... | collective-permute-start | bytes 983048 | tf_op jit(solution)/shard_map/ppermute | solution.py:22
  289.8 9.9 %collective-permute-start.13 = (bf16[4,320,128]{2,1,0:T(8,128)(2,1)}, bf16[4,320,128]{2,1,0:T(8,128)(2,1)}, u32[]{:S(2)}, u32[]{:S(2)}) collective-permute-start(bf16[4,320,128]{2,1,0:T(8,128)(2,1)} %get-tuple-element.14), channel_id=1, source_target_pairs={{1,0},{2,1},{3,2},{4,3},{5,4},{6,5},{7,6},{8,7},{9,8},{10,9},{11,1... | collective-permute-start | bytes 983048 | tf_op jit(solution)/shard_map/ppermute | solution.py:24
  291.9 9.2 %collective-permute-start.12 = (bf16[4,320,128]{2,1,0:T(8,128)(2,1)}, bf16[4,320,128]{2,1,0:T(8,128)(2,1)}, u32[]{:S(2)}, u32[]{:S(2)}) collective-permute-start(bf16[4,320,128]{2,1,0:T(8,128)(2,1)} %get-tuple-element.14), channel_id=1, source_target_pairs={{0,1},{1,2},{2,3},{3,4},{4,5},{5,6},{6,7},{7,8},{8,9},{9,10},{10,1... | collective-permute-start | bytes 983048 | tf_op jit(solution)/shard_map/ppermute | solution.py:22
  306.5 10.2 %collective-permute-start.15 = (bf16[4,320,128]{2,1,0:T(8,128)(2,1)}, bf16[4,320,128]{2,1,0:T(8,128)(2,1)}, u32[]{:S(2)}, u32[]{:S(2)}) collective-permute-start(bf16[4,320,128]{2,1,0:T(8,128)(2,1)} %get-tuple-element.9), channel_id=1, source_target_pairs={{1,0},{2,1},{3,2},{4,3},{5,4},{6,5},{7,6},{8,7},{9,8},{10,9},{11,1... | collective-permute-start | bytes 983048 | tf_op jit(solution)/shard_map/ppermute | solution.py:24
  308.9 9.5 %collective-permute-start.14 = (bf16[4,320,128]{2,1,0:T(8,128)(2,1)}, bf16[4,320,128]{2,1,0:T(8,128)(2,1)}, u32[]{:S(2)}, u32[]{:S(2)}) collective-permute-start(bf16[4,320,128]{2,1,0:T(8,128)(2,1)} %get-tuple-element.9), channel_id=1, source_target_pairs={{0,1},{1,2},{2,3},{3,4},{4,5},{5,6},{6,7},{7,8},{8,9},{9,10},{10,1... | collective-permute-start | bytes 983048 | tf_op jit(solution)/shard_map/ppermute | solution.py:22
  319.8 15.6 %copy-start.34 = (f32[4,320,128]{2,1,0:T(8,128)S(1)}, f32[4,320,128]{2,1,0:T(8,128)}, u32[]{:S(2)}) copy-start(f32[4,320,128]{2,1,0:T(8,128)} %get-tuple-element.11) | copy-start | bytes 1966084
  322.8 7.0 %collective-permute-start.17 = (bf16[4,320,128]{2,1,0:T(8,128)(2,1)S(1)}, bf16[4,320,128]{2,1,0:T(8,128)(2,1)S(1)}, u32[]{:S(2)}, u32[]{:S(2)}) collective-permute-start(bf16[4,320,128]{2,1,0:T(8,128)(2,1)S(1)} %get-tuple-element.4), channel_id=1, source_target_pairs={{1,0},{2,1},{3,2},{4,3},{5,4},{6,5},{7,6},{8,7},{9,8},{10,9},{11,1... | collective-permute-start | bytes 983048 | tf_op jit(solution)/shard_map/ppermute | solution.py:24
  325.2 10.1 %collective-permute-start.16 = (bf16[4,320,128]{2,1,0:T(8,128)(2,1)S(1)}, bf16[4,320,128]{2,1,0:T(8,128)(2,1)S(1)}, u32[]{:S(2)}, u32[]{:S(2)}) collective-permute-start(bf16[4,320,128]{2,1,0:T(8,128)(2,1)S(1)} %get-tuple-element.4), channel_id=1, source_target_pairs={{0,1},{1,2},{2,3},{3,4},{4,5},{5,6},{6,7},{7,8},{8,9},{9,10},{10,1... | collective-permute-start | bytes 983048 | tf_op jit(solution)/shard_map/ppermute | solution.py:22
  342.1 177.5 %reduce-scatter.5.cloned.1.call-start = ((), (), s32[]{:S(2)}) async-start(), calls=%async_computation.5 | async-start | bytes 2949120 | tf_op jit(solution)/shard_map/reduce_scatter | solution.py:134
  (39 other events, 280.0 us)
Sparse Core Ops, SparseCore 0:
  10.6 63.3 all-gather.2
  76.6 62.7 all-gather.4
  342.2 91.0 reduce-scatter.2
  437.3 82.2 reduce-scatter.4
where the time goes:
time: 534 us; the launch traced here: 528 us
  waiting for transfers between devices  330 us (62%)
  other arithmetic  73.8 us (14%)
  local copies, waits for them, and re-layouts  66 us (12%)
  starting transfers between devices  43.2 us (8%)
  between operations  14.7 us (3%)
    reduce_scatter x1, waiting for transfers between devices, body(): lax.psum_scatter(term_vel.astype(jnp.bfloat16), 'shot', scatter_dimension...  90.6 us
    reduce_scatter x1, waiting for transfers between devices, body(): lax.psum_scatter(term_den.astype(jnp.bfloat16), 'shot', scatter_dimension...  84.5 us
    all_gather x1, waiting for transfers between devices, body(): lax.all_gather(den_model, 'shot', axis=0, tiled=True)  65.4 us
    gather x4, local copies, waits for them, and re-layouts, body(): sampled = current.reshape(-1)[station]  64.6 us
    all_gather x1, waiting for transfers between devices, body(): lax.all_gather(vel_model, 'shot', axis=0, tiled=True)  57.9 us
    convert_element_type x8, other arithmetic, field_terms(): field.astype(jnp.bfloat16)  28.6 us
    ppermute x9, starting transfers between devices, padded_2(): lax.ppermute(tail, axis, [(i, (i + 1) % count) for i in range(ends)])  22.9 us
    ppermute x9, waiting for transfers between devices, padded_2(): lax.ppermute(tail, axis, [(i, (i + 1) % count) for i in range(ends)])  22 us
  transfers between devices with their start and end apart: 22, of which 15 were waited for; matrix products, arithmetic and copies ran while one was open for 13% of the time, Pallas kernels for 0%

commit v1 on v0

v1 whole, which is shorter than its diff:
```python
import functools

import jax
import jax.numpy as jnp
import ml_dtypes
import numpy as np
from jax import lax
from jax.experimental import pallas as pl
from jax.experimental.pallas import tpu as pltpu
from jax.sharding import PartitionSpec as P

MESH = pl.DeviceIdType.MESH
BF16 = jnp.bfloat16
F32 = jnp.float32

ITERS = 4
SECOND = (-205.0 / 72.0, 8.0 / 5.0, -1.0 / 5.0, 8.0 / 315.0, -1.0 / 560.0)
FIRST = (4.0 / 5.0, -1.0 / 5.0, 4.0 / 105.0, -1.0 / 280.0)
SECOND_WHOLE = (8064.0, -1008.0, 128.0, -9.0)
FIRST_WHOLE = (672.0, -168.0, 32.0, -3.0)
SPEED = 0.15

PLANES = 4
ROWS = 64
PAD = 16
WINDOW = ROWS + 2 * PAD
LANES = 128
SUB = 16
LOG = 8
DEN, VEL = 0, 1


def band_y():
    taps = np.zeros((2 * ROWS, 2 * WINDOW), np.float32)
    for row in range(ROWS):
        for m in range(1, 5):
            for base in (0, WINDOW):
                taps[row, base + PAD + row + m] = SECOND_WHOLE[m - 1]
                taps[row, base + PAD + row - m] = SECOND_WHOLE[m - 1]
                taps[ROWS + row, base + PAD + row + m] = FIRST_WHOLE[m - 1]
                taps[ROWS + row, base + PAD + row - m] = -FIRST_WHOLE[m - 1]
    return taps.astype(ml_dtypes.bfloat16)


def band_z():
    taps = np.zeros((2 * LANES, 2 * LANES), np.float32)
    for out in range(LANES):
        for m in range(1, 5):
            for base in (0, LANES):
                if out + m < LANES:
                    taps[base + out + m, out] = SECOND_WHOLE[m - 1]
                    taps[base + out + m, LANES + out] = FIRST_WHOLE[m - 1]
                if out - m >= 0:
                    taps[base + out - m, out] = SECOND_WHOLE[m - 1]
                    taps[base + out - m, LANES + out] = -FIRST_WHOLE[m - 1]
    return taps.astype(ml_dtypes.bfloat16)


def kernel(
    n_shot, n_sub, chunks,
    cover, receivers, observed, taps_y, taps_z,
    vel_hbm, den_hbm, p_now, p_before, q_now, q_before,
    grad_vel, grad_den,
    own_tile, left_tile, right_tile, far_tile, pair_tile, pair_out,
    velocity, density, log_den, slopes, high, low, halo, field, adj,
    kept_l, kept_d, count, source, sum_vel, sum_den, y_part, z_part,
    shot_out, shot_pair, far_out, far_in, right_out, left_out, from_left, from_right,
    load_sem, g_send, g_recv, h_send, h_recv, r_send, r_recv,
):
    s = lax.axis_index("shot")
    c = lax.axis_index("sub")
    right = (lax.rem(s + 2, n_shot), c)
    left = (lax.rem(s + n_shot - 2, n_shot), c)
    y_hi = lax.rem(s, 2)
    pair = (s + 1 - 2 * y_hi, c)
    after = (s, c + 1)
    before = (s, c - 1)
    has_after = c < n_sub - 1
    has_before = c > 0

    loads = [
        pltpu.make_async_copy(den_hbm.at[0], own_tile.at[DEN], load_sem.at[0]),
        pltpu.make_async_copy(vel_hbm.at[0], own_tile.at[VEL], load_sem.at[1]),
        pltpu.make_async_copy(p_now.at[0], field.at[0], load_sem.at[2]),
        pltpu.make_async_copy(p_before.at[0], field.at[1], load_sem.at[3]),
        pltpu.make_async_copy(q_now.at[0], adj.at[0], load_sem.at[4]),
        pltpu.make_async_copy(q_before.at[0], adj.at[1], load_sem.at[5]),
    ]
    for load in loads:
        load.start()

    barrier = pltpu.get_barrier_semaphore()
    for other in (right, left, pair):
        pl.semaphore_signal(barrier, 1, device_id=other, device_id_type=MESH)

    @pl.when(has_after)
    def _():
        pl.semaphore_signal(barrier, 1, device_id=after, device_id_type=MESH)

    @pl.when(has_before)
    def _():
        pl.semaphore_signal(barrier, 1, device_id=before, device_id_type=MESH)

    mine = cover[s, c]
    theirs = cover[pair[0], c]

    def row_of(step):
        return lax.rem(s + 2 * step, n_shot)

    def flag(test):
        return jnp.where(test, 1.0, 0.0).astype(F32)

    steps = (0, 3, 1, 2)
    mine_is = [flag(mine == row_of(k)) for k in steps]
    theirs_is = [flag(theirs == row_of(k)) for k in steps]
    mine_pair = flag(lax.rem(mine, 2) != y_hi)

    def rows(chunk, group=None):
        if group is None:
            return pl.ds(pl.multiple_of(chunk * ROWS, ROWS), ROWS)
        return pl.ds(pl.multiple_of(chunk * ROWS + group * SUB, SUB), SUB)

    def padded(chunk, group=None):
        if group is None:
            return pl.ds(pl.multiple_of(chunk * ROWS + PAD, SUB), ROWS)
        return pl.ds(pl.multiple_of(chunk * ROWS + group * SUB + PAD, SUB), SUB)

    low_half, high_half = pl.ds(0, 2), pl.ds(2, 2)
    every = pl.ds(0, PLANES)

    def g_copy(kind, a, chunk):
        part = rows(chunk)
        if kind == 0:
            src, dst, to = own_tile.at[a, every, part], left_tile.at[a, every, part], right
        elif kind == 1:
            src, dst, to = own_tile.at[a, every, part], right_tile.at[a, every, part], left
        elif kind == 2:
            src, dst, to = left_tile.at[a, low_half, part], far_tile.at[a, low_half, part], right
        elif kind == 3:
            src, dst, to = right_tile.at[a, high_half, part], far_tile.at[a, high_half, part], left
        else:
            src, dst, to = pair_out.at[a, every, part], pair_tile.at[a, every, part], pair
        return pltpu.make_async_remote_copy(
            src_ref=src, dst_ref=dst, send_sem=g_send.at[a, chunk, kind],
            recv_sem=g_recv.at[a, chunk, kind], device_id=to, device_id_type=MESH,
        )

    def h_copy(side, slot, e, chunk):
        return pltpu.make_async_remote_copy(
            src_ref=high.at[slot, every, padded(chunk)],
            dst_ref=halo.at[e, side, every, rows(chunk)],
            send_sem=h_send.at[e, chunk, side], recv_sem=h_recv.at[e, chunk, side],
            device_id=after if side == 0 else before, device_id_type=MESH,
        )

    def h_start(slot, e, chunk):
        @pl.when(has_after)
        def _():
            h_copy(0, slot, e, chunk).start()

        @pl.when(has_before)
        def _():
            h_copy(1, slot, e, chunk).start()

    def h_wait_recv(slot, e, chunk):
        @pl.when(has_before)
        def _():
            h_copy(0, slot, e, chunk).wait_recv()

        @pl.when(has_after)
        def _():
            h_copy(1, slot, e, chunk).wait_recv()

    def h_wait_send(slot, e, chunk):
        @pl.when(has_after)
        def _():
            h_copy(0, slot, e, chunk).wait_send()

        @pl.when(has_before)
        def _():
            h_copy(1, slot, e, chunk).wait_send()

    def r_copy(kind, b, chunk):
        part = rows(chunk)
        if kind == 0:
            src, dst, to = shot_out.at[b, every, part], shot_pair.at[b, every, part], pair
        elif kind == 1:
            src, dst, to = far_out.at[b, low_half, part], far_in.at[b, low_half, part], right
        elif kind == 2:
            src, dst, to = far_out.at[b, high_half, part], far_in.at[b, high_half, part], left
        elif kind == 3:
            src, dst, to = right_out.at[b, every, part], from_left.at[b, every, part], right
        else:
            src, dst, to = left_out.at[b, every, part], from_right.at[b, every, part], left
        return pltpu.make_async_remote_copy(
            src_ref=src, dst_ref=dst, send_sem=r_send.at[b, chunk, kind],
            recv_sem=r_recv.at[b, chunk, kind], device_id=to, device_id_type=MESH,
        )

    def put_split(slot, chunk, group, value):
        top = value.astype(BF16)
        high[slot, :, padded(chunk, group), :] = top
        low[slot, :, padded(chunk, group), :] = (value - top.astype(F32)).astype(BF16)

    def matrix_part(slot, chunk):
        window = pl.ds(pl.multiple_of(chunk * ROWS, ROWS), WINDOW)
        columns = jnp.concatenate(
            [
                jnp.concatenate([ref[slot, plane, window, :] for plane in range(PLANES)], axis=1)
                for ref in (high, low)
            ],
            axis=0,
        )
        y_part[...] = jnp.dot(taps_y[...], columns, preferred_element_type=F32)
        lines = jnp.concatenate(
            [
                jnp.concatenate(
                    [high[slot, plane, padded(chunk), :], low[slot, plane, padded(chunk), :]], axis=1
                )
                for plane in range(PLANES)
            ],
            axis=0,
        )
        z_part[...] = jnp.dot(lines, taps_z[...], preferred_element_type=F32)

    def from_y(group, second):
        part = pl.ds((0 if second else ROWS) + group * SUB, SUB)
        return jnp.stack(
            [y_part[part, pl.ds(plane * LANES, LANES)] for plane in range(PLANES)], axis=0
        )

    def from_z(group, second):
        lanes = pl.ds(0 if second else LANES, LANES)
        return jnp.stack(
            [z_part[pl.ds(plane * ROWS + group * SUB, SUB), lanes] for plane in range(PLANES)],
            axis=0,
        )

    def vector_part(own, e, chunk, group, second):
        wide = jnp.concatenate(
            [
                halo[e, 0, :, rows(chunk, group), :].astype(F32),
                own,
                halo[e, 1, :, rows(chunk, group), :].astype(F32),
            ],
            axis=0,
        )
        d_x = None
        laplace = (3.0 * SECOND[0]) * own if second else None
        for m in range(1, 5):
            up, down = wide[4 + m : 8 + m], wide[4 - m : 8 - m]
            term = FIRST[m - 1] * (up - down)
            d_x = term if d_x is None else d_x + term
            if second:
                laplace = laplace + SECOND[m] * (up + down)
        d_y = from_y(group, False) * (1.0 / 840.0)
        d_z = from_z(group, False) * (1.0 / 840.0)
        if second:
            laplace = laplace + (from_y(group, True) + from_z(group, True)) * (1.0 / 5040.0)
        return laplace, (d_x, d_y, d_z)

    groups = ROWS // SUB

    def operate(laplace, diffs, chunk, group):
        part = rows(chunk, group)
        return laplace - (
            slopes[0, :, part, :] * diffs[0]
            + slopes[1, :, part, :] * diffs[1]
            + slopes[2, :, part, :] * diffs[2]
        )

    def take_tile(a, chunk):
        for kind in (0, 1):
            g_copy(kind, a, chunk).start()

    def relay_tile(a, chunk):
        g_copy(0, a, chunk).wait_recv()
        g_copy(2, a, chunk).start()
        g_copy(1, a, chunk).wait_recv()
        g_copy(3, a, chunk).start()

    def chosen(a, part, flags):
        total = own_tile[a, :, part, :].astype(F32) * flags[0]
        for ref, one in zip((left_tile, right_tile, far_tile), flags[1:]):
            total = total + ref[a, :, part, :].astype(F32) * one
        return total

    def pair_tile_send(a, chunk):
        g_copy(2, a, chunk).wait_recv()
        g_copy(3, a, chunk).wait_recv()
        for group in range(groups):
            part = rows(chunk, group)
            pair_out[a, :, part, :] = chosen(a, part, theirs_is).astype(BF16)
        g_copy(4, a, chunk).start()

    def finish_density(chunk):
        g_copy(4, DEN, chunk).wait_recv()
        for group in range(groups):
            part = rows(chunk, group)
            value = chosen(DEN, part, mine_is) + pair_tile[DEN, :, part, :].astype(F32) * mine_pair
            density[:, part, :] = value
            logs = jnp.log(value)
            log_den[:, part, :] = logs
            put_split(2, chunk, group, logs)
        h_start(2, LOG, chunk)

    def finish_velocity(chunk):
        g_copy(4, VEL, chunk).wait_recv()
        for group in range(groups):
            part = rows(chunk, group)
            velocity[:, part, :] = (
                chosen(VEL, part, mine_is) + pair_tile[VEL, :, part, :].astype(F32) * mine_pair
            )

    def make_slopes(chunk):
        h_wait_recv(2, LOG, chunk)
        matrix_part(2, chunk)
        for group in range(groups):
            part = rows(chunk, group)
            _, diffs = vector_part(log_den[:, part, :], LOG, chunk, group, False)
            for d in range(3):
                slopes[d, :, part, :] = diffs[d]

    def forward(chunk, n):
        now, other = lax.rem(n, 2), lax.rem(n + 1, 2)
        h_wait_recv(now, n, chunk)
        matrix_part(now, chunk)

        @pl.when(n > 0)
        def _():
            h_wait_send(other, n - 1, chunk)

        last = n == ITERS - 1
        for group in range(groups):
            part = rows(chunk, group)
            own = field[now, :, part, :]
            laplace, diffs = vector_part(own, n, chunk, group, True)
            applied = operate(laplace, diffs, chunk, group)
            kept_l[n, :, part, :] = applied
            for d in range(3):
                kept_d[n, d, :, part, :] = diffs[d]
            vel = velocity[:, part, :]
            moved = 2.0 * own - field[other, :, part, :] + (SPEED * vel * vel) * applied
            misfit = count[:, part, :] * moved - source[n, :, part, :]
            source[n, :, part, :] = misfit
            following = jnp.where(last, adj[0, :, part, :] + misfit, moved)
            field[other, :, part, :] = following
            put_split(other, chunk, group, following)
        h_start(other, n + 1, chunk)

    def backward(chunk, n):
        now, other = lax.rem(n, 2), lax.rem(n + 1, 2)
        k = n - ITERS
        h_wait_recv(now, n, chunk)
        matrix_part(now, chunk)
        h_wait_send(other, n - 1, chunk)
        for group in range(groups):
            part = rows(chunk, group)
            own = field[now, :, part, :]
            laplace, diffs = vector_part(own, n, chunk, group, True)
            applied = operate(laplace, diffs, chunk, group)
            vel = velocity[:, part, :]
            moved = 2.0 * own - adj[other, :, part, :] + (SPEED * vel * vel) * applied
            adj[other, :, part, :] = moved
            following = moved + source[2 - k, :, part, :]
            field[other, :, part, :] = following
            put_split(other, chunk, group, following)
            total = sum_vel[:, part, :] + own * kept_l[3 - k, :, part, :]
            sum_vel[:, part, :] = total
            sum_den[:, part, :] += (
                diffs[0] * kept_d[3 - k, 0, :, part, :]
                + diffs[1] * kept_d[3 - k, 1, :, part, :]
                + diffs[2] * kept_d[3 - k, 2, :, part, :]
            )

            @pl.when(k == 2)
            def _():
                whole = total + following * kept_l[0, :, part, :]
                shot_out[VEL, :, part, :] = (2.0 * SPEED * vel * whole).astype(BF16)

        h_start(other, n + 1, chunk)

        @pl.when(k == 2)
        def _():
            r_copy(0, VEL, chunk).start()

    def backward_last(chunk):
        n = 2 * ITERS - 1
        h_wait_recv(n % 2, n, chunk)
        matrix_part(n % 2, chunk)
        for group in range(groups):
            part = rows(chunk, group)
            own = field[n % 2, :, part, :]
            _, diffs = vector_part(own, n, chunk, group, False)
            whole = sum_den[:, part, :] + (
                diffs[0] * kept_d[0, 0, :, part, :]
                + diffs[1] * kept_d[0, 1, :, part, :]
                + diffs[2] * kept_d[0, 2, :, part, :]
            )
            vel = velocity[:, part, :]
            shot_out[DEN, :, part, :] = (
                (SPEED * vel * vel) / density[:, part, :] * whole
            ).astype(BF16)
        r_copy(0, DEN, chunk).start()

    def for_step(b, part, which):
        return (
            shot_out[b, :, part, :].astype(F32) * mine_is[which]
            + shot_pair[b, :, part, :].astype(F32) * theirs_is[which]
        )

    def reduce_far(b, chunk):
        r_copy(0, b, chunk).wait_recv()
        for group in range(groups):
            part = rows(chunk, group)
            far_out[b, :, part, :] = for_step(b, part, 3).astype(BF16)
        r_copy(1, b, chunk).start()
        r_copy(2, b, chunk).start()

    def reduce_near(b, chunk):
        r_copy(1, b, chunk).wait_recv()
        r_copy(2, b, chunk).wait_recv()
        for group in range(groups):
            part = rows(chunk, group)
            arrived = far_in[b, :, part, :].astype(F32)
            to_right = for_step(b, part, 2)
            to_left = for_step(b, part, 1)
            right_out[b, 0:2, part, :] = (to_right[0:2] + arrived[0:2]).astype(BF16)
            right_out[b, 2:4, part, :] = to_right[2:4].astype(BF16)
            left_out[b, 0:2, part, :] = to_left[0:2].astype(BF16)
            left_out[b, 2:4, part, :] = (to_left[2:4] + arrived[2:4]).astype(BF16)
        r_copy(3, b, chunk).start()
        r_copy(4, b, chunk).start()

    def reduce_end(b, chunk):
        r_copy(3, b, chunk).wait_recv()
        r_copy(4, b, chunk).wait_recv()
        out = grad_vel if b == VEL else grad_den
        for group in range(groups):
            part = rows(chunk, group)
            out[0, :, part, :] = (
                for_step(b, part, 0)
                + from_left[b, :, part, :].astype(F32)
                + from_right[b, :, part, :].astype(F32)
            )

    loads[0].wait()
    loads[1].wait()

    barrier_count = 3 + has_after.astype(jnp.int32) + has_before.astype(jnp.int32)
    pl.semaphore_wait(barrier, barrier_count)

    take_tile(DEN, 0)
    take_tile(VEL, 0)

    edge = jnp.zeros((3, PLANES, PAD, LANES), BF16)
    for ref in (high, low):
        ref[:, :, 0:PAD, :] = edge
        ref[:, :, PAD + chunks * ROWS :, :] = edge

    def clear_side(side):
        def clear(i, _):
            halo[i, side] = jnp.zeros((PLANES, chunks * ROWS, LANES), BF16)
            return 0

        lax.fori_loop(0, 9, clear, 0)

    pl.when(c == 0)(lambda: clear_side(0))
    pl.when(c == n_sub - 1)(lambda: clear_side(1))

    loads[2].wait()

    def first_field(chunk, _):
        for group in range(groups):
            put_split(0, chunk, group, field[0, :, rows(chunk, group), :])
        h_start(0, 0, chunk)
        return 0

    lax.fori_loop(0, chunks, first_field, 0)

    place = receivers[...] - c * (PLANES * chunks * ROWS * LANES)
    line = lax.shift_right_arithmetic(place, 7)
    lane = place & (LANES - 1)
    n_rec = receivers.shape[1]
    at_lane = (lax.broadcasted_iota(jnp.int32, (LANES, n_rec), 0) == lane).astype(F32)
    at_lane_16 = at_lane.astype(BF16)
    seen = []
    for n in range(ITERS):
        values = at_lane * observed[0, n : n + 1, :]
        top = values.astype(BF16)
        seen.append(jnp.concatenate([top, (values - top.astype(F32)).astype(BF16)], axis=1))
    contract = (((1,), (1,)), ((), ()))

    def receivers_of_plane(plane, _):
        lines = lax.broadcasted_iota(jnp.int32, (chunks * ROWS, n_rec), 0) + plane * (chunks * ROWS)
        at_line = (lines == line).astype(F32).astype(BF16)
        count[plane] = lax.dot_general(at_line, at_lane_16, contract, preferred_element_type=F32)
        twice = jnp.concatenate([at_line, at_line], axis=1)
        for n in range(ITERS):
            source[n, plane] = lax.dot_general(twice, seen[n], contract, preferred_element_type=F32)
        return 0

    lax.fori_loop(0, PLANES, receivers_of_plane, 0)

    def clear_sums(plane, _):
        sum_vel[plane] = jnp.zeros((chunks * ROWS, LANES), F32)
        sum_den[plane] = jnp.zeros((chunks * ROWS, LANES), F32)
        return 0

    lax.fori_loop(0, PLANES, clear_sums, 0)

    for load in loads[3:]:
        load.wait()

    def at(chunk, event):
        pl.when(jnp.logical_and(chunk >= 0, chunk < chunks))(lambda: event(chunk))

    first_wave = 3
    n_waves = chunks + 2 * ITERS - 1
    ticks = first_wave + n_waves + 4

    def tick(t, _):
        def next_tiles(chunk):
            take_tile(DEN, chunk)
            take_tile(VEL, chunk)

        def relays(chunk):
            relay_tile(DEN, chunk)
            relay_tile(VEL, chunk)

        def pairs(chunk):
            pair_tile_send(DEN, chunk)
            pair_tile_send(VEL, chunk)

        def finish(chunk):
            finish_density(chunk)
            finish_velocity(chunk)

        at(t + 1, next_tiles)
        at(t, relays)
        at(t, pairs)
        at(t - 1, finish)
        wave = t - first_wave
        at(wave, make_slopes)

        def reduce_lag(b, wave_of):
            at(wave - wave_of - 1, functools.partial(reduce_far, b))
            at(wave - wave_of - 2, functools.partial(reduce_near, b))
            at(wave - wave_of - 4, functools.partial(reduce_end, b))

        reduce_lag(VEL, 6)
        reduce_lag(DEN, 7)

        def process(n, _):
            chunk = wave - n
            pl.when(n < ITERS)(lambda: forward(chunk, n))
            pl.when(jnp.logical_and(n >= ITERS, n < 2 * ITERS - 1))(lambda: backward(chunk, n))
            pl.when(n == 2 * ITERS - 1)(lambda: backward_last(chunk))
            return 0

        lax.fori_loop(
            jnp.maximum(wave - (chunks - 1), 0), jnp.minimum(wave + 1, 2 * ITERS), process, 0
        )
        return 0

    lax.fori_loop(0, ticks, tick, 0)

    def drain(chunk, _):
        for a in range(2):
            for kind in range(5):
                g_copy(kind, a, chunk).wait_send()
                r_copy(kind, a, chunk).wait_send()
        h_wait_send(0, 6, chunk)
        h_wait_send(1, 7, chunk)
        h_wait_send(2, LOG, chunk)
        return 0

    lax.fori_loop(0, chunks, drain, 0)


def body(vel_model, den_model, cover, receivers, observed, p_now, p_before, q_now, q_before):
    n_shot, n_sub = lax.axis_size("shot"), lax.axis_size("sub")
    _, planes, length, lanes = vel_model.shape
    chunks = length // ROWS
    tile = (planes, length, lanes)
    tall = (planes, length + 2 * PAD, lanes)
    vmem = pl.BlockSpec(memory_space=pltpu.VMEM)
    anywhere = pl.BlockSpec(memory_space=pl.ANY)
    out = jax.ShapeDtypeStruct((1, *tile), F32)
    return pl.pallas_call(
        functools.partial(kernel, n_shot, n_sub, chunks),
        name="window",
        out_shape=(out, out),
        in_specs=[pl.BlockSpec(memory_space=pltpu.SMEM)] + [vmem] * 4 + [anywhere] * 6,
        out_specs=(vmem, vmem),
        scratch_shapes=[
            *[pltpu.VMEM((2, *tile), BF16) for _ in range(6)],
            pltpu.VMEM(tile, F32),
            pltpu.VMEM(tile, F32),
            pltpu.VMEM(tile, F32),
            pltpu.VMEM((3, *tile), F32),
            pltpu.VMEM((3, *tall), BF16),
            pltpu.VMEM((3, *tall), BF16),
            pltpu.VMEM((9, 2, *tile), BF16),
            pltpu.VMEM((2, *tile), F32),
            pltpu.VMEM((2, *tile), F32),
            pltpu.VMEM((ITERS, *tile), F32),
            pltpu.VMEM((ITERS, 3, *tile), F32),
            pltpu.VMEM(tile, F32),
            pltpu.VMEM((ITERS, *tile), F32),
            pltpu.VMEM(tile, F32),
            pltpu.VMEM(tile, F32),
            pltpu.VMEM((2 * ROWS, PLANES * LANES), F32),
            pltpu.VMEM((PLANES * ROWS, 2 * LANES), F32),
            *[pltpu.VMEM((2, *tile), BF16) for _ in range(8)],
            pltpu.SemaphoreType.DMA((6,)),
            pltpu.SemaphoreType.DMA((2, chunks, 5)),
            pltpu.SemaphoreType.DMA((2, chunks, 5)),
            pltpu.SemaphoreType.DMA((9, chunks, 2)),
            pltpu.SemaphoreType.DMA((9, chunks, 2)),
            pltpu.SemaphoreType.DMA((2, chunks, 5)),
            pltpu.SemaphoreType.DMA((2, chunks, 5)),
        ],
        compiler_params=pltpu.CompilerParams(
            collective_id=0, has_side_effects=True, vmem_limit_bytes=60 * 1024 * 1024
        ),
    )(
        cover, receivers, observed, jnp.asarray(band_y()), jnp.asarray(band_z()),
        vel_model, den_model, p_now, p_before, q_now, q_before,
    )


def solution(mesh):
    tiles = P("shot", "sub", None, None)
    return jax.shard_map(
        body,
        mesh=mesh,
        in_specs=(
            tiles, tiles, P(), P("shot", None), P("shot", None, None), tiles, tiles, tiles, tiles,
        ),
        out_specs=(tiles, tiles),
        check_vma=False,
    )
```

time: 534 us -> 120 us (0.22)
  waiting for transfers between devices: 330 us -> 0 us
  Pallas kernels: 0 us -> 115 us
  other arithmetic: 73.8 us -> 0 us
  local copies, waits for them, and re-layouts: 66 us -> 2.87 us
  starting transfers between devices: 43.2 us -> 0 us
  between operations: 14.7 us -> 0.65 us
    reduce_scatter x2 -> x0, waiting for transfers between devices: 175 us -> none  [the longest x1 90.6 us: body(): lax.psum_scatter(term_vel.astype(jnp.bfloat16), 'shot', scatter_dimension...]
    all_gather x2 -> x0, waiting for transfers between devices: 123 us -> none  [the longest x1 65.4 us: body(): lax.all_gather(den_model, 'shot', axis=0, tiled=True)]
    pallas_call x0 -> x1, Pallas kernels: none -> 115 us  [body(): pl.pallas_call(functools.partial(kernel, n_shot, n_sub, chunks), name='wi...]
    gather x4 -> x0, local copies, waits for them, and re-layouts: 64.6 us -> none  [body(): sampled = current.reshape(-1)[station]]
    convert_element_type x23 -> x0, other arithmetic: 46.6 us -> none  [the longest x8 28.6 us: field_terms(): field.astype(jnp.bfloat16)]
    ppermute x18 -> x0, starting transfers between devices: 43.1 us -> none  [the longest x9 22.9 us: padded_2(): lax.ppermute(tail, axis, [(i, (i + 1) % count) for i in range(ends)])]
    ppermute x18 -> x0, waiting for transfers between devices: 29.9 us -> none  [the longest x9 22 us: padded_2(): lax.ppermute(tail, axis, [(i, (i + 1) % count) for i in range(ends)])]
    scatter-add x4 -> x0, other arithmetic: 18.8 us -> none  [body(): source = jnp.zeros((cells,), jnp.float32).at[station].add(misfits[ITERS -...]
  transfers between devices with their start and end apart: 22 -> 0, of which waited for: 15 -> 0; matrix products, arithmetic and copies ran while one was open for 13% -> 0% of each run, Pallas kernels for 0% -> 0%
where the time goes in v1:
time: 120 us; the launch traced here: 118 us
  Pallas kernels  115 us (96%)
  local copies, waits for them, and re-layouts  2.87 us (2%)
    pallas_call x1, Pallas kernels, body(): pl.pallas_call(functools.partial(kernel, n_shot, n_sub, chunks), name='wi...  115 us
    unnamed x4, local copies, waits for them, and re-layouts  2.87 us

profile of v1, /device:TPU:232, one launch (start us, length us, event | category | flops | bytes accessed | tf_op | source)
XLA Modules:
  0.0 118.2 jit_solution(17263398528027161118)
XLA Ops:
  0.6 114.7 %window.1 = (f32[1,4,320,128]{3,2,1,0:T(8,128)}, f32[1,4,320,128]{3,2,1,0:T(8,128)}) custom-call(s32[8,32]{1,0:T(8,128)} %cover.1, s32[1,512]{1,0:T(1,128)} %receivers.1, f32[1,4,512]{2,1,0:T(4,128)} %observed.1, bf16[128,192]{1,0:T(8,128)(2,1)} %constant.4.clone.taps_y, bf16[256,256]{1,0:T(8,128)(2,1)} %constant.5.clone.taps_z, ...), custom_call_target="tpu_custom_call" | custom-call | tf_op jit(solution)/shard_map/window/pallas_call | solution.py:590
  115.3 0.0 copy-start
  115.4 2.0 %copy.15 = f32[1,4,320,128]{3,2,1,0:T(8,128)} copy(f32[1,4,320,128]{3,2,1,0:T(8,128)} %get-tuple-element.4) | data formatting | bytes 1310720
  117.4 0.0 copy-done
  117.4 0.8 copy.16
Async XLA Ops:
  115.3 2.0 %copy-start = (f32[1,4,320,128]{3,2,1,0:T(8,128)S(1)}, f32[1,4,320,128]{3,2,1,0:T(8,128)}, u32[]{:S(2)}) copy-start(f32[1,4,320,128]{3,2,1,0:T(8,128)} %get-tuple-element.5) | copy-start | bytes 1966084

commit v2 on v1

--- a/solution.py
+++ b/solution.py
@@ -65,7 +65,7 @@
     velocity, density, log_den, slopes, high, low, halo, field, adj,
     kept_l, kept_d, count, source, sum_vel, sum_den, y_part, z_part,
     shot_out, shot_pair, far_out, far_in, right_out, left_out, from_left, from_right,
-    load_sem, g_send, g_recv, h_send, h_recv, r_send, r_recv,
+    spot, seen, load_sem, g_send, g_recv, h_send, h_recv, r_send, r_recv,
 ):
     s = lax.axis_index("shot")
     c = lax.axis_index("sub")
@@ -450,8 +450,9 @@
     barrier_count = 3 + has_after.astype(jnp.int32) + has_before.astype(jnp.int32)
     pl.semaphore_wait(barrier, barrier_count)
 
-    take_tile(DEN, 0)
-    take_tile(VEL, 0)
+    for chunk in range(2):
+        take_tile(DEN, chunk)
+        take_tile(VEL, chunk)
 
     edge = jnp.zeros((3, PLANES, PAD, LANES), BF16)
     for ref in (high, low):
@@ -478,29 +479,31 @@
 
     lax.fori_loop(0, chunks, first_field, 0)
 
-    place = receivers[...] - c * (PLANES * chunks * ROWS * LANES)
-    line = lax.shift_right_arithmetic(place, 7)
-    lane = place & (LANES - 1)
+    cells = PLANES * chunks * ROWS * LANES
     n_rec = receivers.shape[1]
-    at_lane = (lax.broadcasted_iota(jnp.int32, (LANES, n_rec), 0) == lane).astype(F32)
-    at_lane_16 = at_lane.astype(BF16)
-    seen = []
-    for n in range(ITERS):
-        values = at_lane * observed[0, n : n + 1, :]
-        top = values.astype(BF16)
-        seen.append(jnp.concatenate([top, (values - top.astype(F32)).astype(BF16)], axis=1))
+
+    def receiver_lanes():
+        lane = (receivers[...] - c * cells) & (LANES - 1)
+        at_lane = (lax.broadcasted_iota(jnp.int32, (LANES, n_rec), 0) == lane).astype(F32)
+        spot[...] = at_lane.astype(BF16)
+        for n in range(ITERS):
+            values = at_lane * observed[0, n : n + 1, :]
+            top = values.astype(BF16)
+            seen[n, :, 0:n_rec] = top
+            seen[n, :, n_rec : 2 * n_rec] = (values - top.astype(F32)).astype(BF16)
+
     contract = (((1,), (1,)), ((), ()))
 
-    def receivers_of_plane(plane, _):
+    def receivers_of_plane(plane):
+        line = lax.shift_right_arithmetic(receivers[...] - c * cells, 7)
         lines = lax.broadcasted_iota(jnp.int32, (chunks * ROWS, n_rec), 0) + plane * (chunks * ROWS)
         at_line = (lines == line).astype(F32).astype(BF16)
-        count[plane] = lax.dot_general(at_line, at_lane_16, contract, preferred_element_type=F32)
+        count[plane] = lax.dot_general(at_line, spot[...], contract, preferred_element_type=F32)
         twice = jnp.concatenate([at_line, at_line], axis=1)
         for n in range(ITERS):
-            source[n, plane] = lax.dot_general(twice, seen[n], contract, preferred_element_type=F32)
-        return 0
-
-    lax.fori_loop(0, PLANES, receivers_of_plane, 0)
+            source[n, plane] = lax.dot_general(
+                twice, seen[n], contract, preferred_element_type=F32
+            )
 
     def clear_sums(plane, _):
         sum_vel[plane] = jnp.zeros((chunks * ROWS, LANES), F32)
@@ -508,6 +511,7 @@
         return 0
 
     lax.fori_loop(0, PLANES, clear_sums, 0)
+    receiver_lanes()
 
     for load in loads[3:]:
         load.wait()
@@ -520,6 +524,10 @@
     ticks = first_wave + n_waves + 4
 
     def tick(t, _):
+        def plane_pair(pair_index):
+            receivers_of_plane(2 * pair_index)
+            receivers_of_plane(2 * pair_index + 1)
+
         def next_tiles(chunk):
             take_tile(DEN, chunk)
             take_tile(VEL, chunk)
@@ -536,10 +544,11 @@
             finish_density(chunk)
             finish_velocity(chunk)
 
-        at(t + 1, next_tiles)
         at(t, relays)
-        at(t, pairs)
-        at(t - 1, finish)
+        at(t + 2, next_tiles)
+        at(t - 1, pairs)
+        at(t - 2, finish)
+        pl.when(t < 2)(lambda: plane_pair(t))
         wave = t - first_wave
         at(wave, make_slopes)
 
@@ -547,9 +556,6 @@
             at(wave - wave_of - 1, functools.partial(reduce_far, b))
             at(wave - wave_of - 2, functools.partial(reduce_near, b))
             at(wave - wave_of - 4, functools.partial(reduce_end, b))
-
-        reduce_lag(VEL, 6)
-        reduce_lag(DEN, 7)
 
         def process(n, _):
             chunk = wave - n
@@ -561,6 +567,8 @@
         lax.fori_loop(
             jnp.maximum(wave - (chunks - 1), 0), jnp.minimum(wave + 1, 2 * ITERS), process, 0
         )
+        reduce_lag(VEL, 6)
+        reduce_lag(DEN, 7)
         return 0
 
     lax.fori_loop(0, ticks, tick, 0)
@@ -613,6 +621,8 @@
             pltpu.VMEM((2 * ROWS, PLANES * LANES), F32),
             pltpu.VMEM((PLANES * ROWS, 2 * LANES), F32),
             *[pltpu.VMEM((2, *tile), BF16) for _ in range(8)],
+            pltpu.VMEM((LANES, receivers.shape[1]), BF16),
+            pltpu.VMEM((ITERS, LANES, 2 * receivers.shape[1]), BF16),
             pltpu.SemaphoreType.DMA((6,)),
             pltpu.SemaphoreType.DMA((2, chunks, 5)),
             pltpu.SemaphoreType.DMA((2, chunks, 5)),

time: 120 us -> 102 us (0.85); the launches traced: 118 us -> 102 us
  Pallas kernels: 115 us -> 98 us
    pallas_call x1, Pallas kernels: 115 us -> 98 us  [body(): pl.pallas_call(functools.partial(kernel, n_shot, n_sub, chunks), name='wi...]
where the time goes in v2:
time: 102 us
  Pallas kernels  98 us (96%)
  local copies, waits for them, and re-layouts  2.87 us (3%)
    pallas_call x1, Pallas kernels, body(): pl.pallas_call(functools.partial(kernel, n_shot, n_sub, chunks), name='wi...  98 us
    unnamed x4, local copies, waits for them, and re-layouts  2.87 us

profile of v2, /device:TPU:232, one launch (start us, length us, event | category | flops | bytes accessed | tf_op | source)
XLA Modules:
  0.0 101.5 jit_solution(10007103724400787607)
XLA Ops:
  0.6 98.0 %window.1 = (f32[1,4,320,128]{3,2,1,0:T(8,128)}, f32[1,4,320,128]{3,2,1,0:T(8,128)}) custom-call(s32[8,32]{1,0:T(8,128)} %cover.1, s32[1,512]{1,0:T(1,128)} %receivers.1, f32[1,4,512]{2,1,0:T(4,128)} %observed.1, bf16[128,192]{1,0:T(8,128)(2,1)} %constant.4.clone.taps_y, bf16[256,256]{1,0:T(8,128)(2,1)} %constant.5.clone.taps_z, ...), custom_call_target="tpu_custom_call" | custom-call | tf_op jit(solution)/shard_map/window/pallas_call | solution.py:598
  98.6 0.0 copy-start
  98.6 2.0 %copy.15 = f32[1,4,320,128]{3,2,1,0:T(8,128)} copy(f32[1,4,320,128]{3,2,1,0:T(8,128)} %get-tuple-element.4) | data formatting | bytes 1310720
  100.7 0.0 copy-done
  100.7 0.8 copy.16
Async XLA Ops:
  98.6 2.0 %copy-start = (f32[1,4,320,128]{3,2,1,0:T(8,128)S(1)}, f32[1,4,320,128]{3,2,1,0:T(8,128)}, u32[]{:S(2)}) copy-start(f32[1,4,320,128]{3,2,1,0:T(8,128)} %get-tuple-element.5) | copy-start | bytes 1966084

commit v3 on v2

--- a/solution.py
+++ b/solution.py
@@ -64,7 +64,7 @@
     own_tile, left_tile, right_tile, far_tile, pair_tile, pair_out,
     velocity, density, log_den, slopes, high, low, halo, field, adj,
     kept_l, kept_d, count, source, sum_vel, sum_den, y_part, z_part,
-    shot_out, shot_pair, far_out, far_in, right_out, left_out, from_left, from_right,
+    shot_out, shot_pair, far_out, far_in, right_out, left_out, near_in,
     spot, seen, load_sem, g_send, g_recv, h_send, h_recv, r_send, r_recv,
 ):
     s = lax.axis_index("shot")
@@ -128,57 +128,81 @@
     low_half, high_half = pl.ds(0, 2), pl.ds(2, 2)
     every = pl.ds(0, PLANES)
 
-    def g_copy(kind, a, chunk):
+    both = pl.ds(0, 2)
+
+    def remote(src, dst, send, recv, to):
+        return pltpu.make_async_remote_copy(
+            src_ref=src, dst_ref=dst, send_sem=send, recv_sem=recv, device_id=to, device_id_type=MESH
+        )
+
+    def g_copy(kind, chunk):
         part = rows(chunk)
         if kind == 0:
-            src, dst, to = own_tile.at[a, every, part], left_tile.at[a, every, part], right
+            src, dst, to = own_tile.at[both, every, part], left_tile.at[both, every, part], right
         elif kind == 1:
-            src, dst, to = own_tile.at[a, every, part], right_tile.at[a, every, part], left
+            src, dst, to = own_tile.at[both, every, part], right_tile.at[both, every, part], left
         elif kind == 2:
-            src, dst, to = left_tile.at[a, low_half, part], far_tile.at[a, low_half, part], right
+            src, dst, to = (
+                left_tile.at[both, low_half, part], far_tile.at[both, low_half, part], right
+            )
         elif kind == 3:
-            src, dst, to = right_tile.at[a, high_half, part], far_tile.at[a, high_half, part], left
+            src, dst, to = (
+                right_tile.at[both, high_half, part], far_tile.at[both, high_half, part], left
+            )
         else:
-            src, dst, to = pair_out.at[a, every, part], pair_tile.at[a, every, part], pair
-        return pltpu.make_async_remote_copy(
-            src_ref=src, dst_ref=dst, send_sem=g_send.at[a, chunk, kind],
-            recv_sem=g_recv.at[a, chunk, kind], device_id=to, device_id_type=MESH,
-        )
-
-    def h_copy(side, slot, e, chunk):
-        return pltpu.make_async_remote_copy(
-            src_ref=high.at[slot, every, padded(chunk)],
-            dst_ref=halo.at[e, side, every, rows(chunk)],
-            send_sem=h_send.at[e, chunk, side], recv_sem=h_recv.at[e, chunk, side],
-            device_id=after if side == 0 else before, device_id_type=MESH,
-        )
-
-    def h_start(slot, e, chunk):
+            src, dst, to = pair_out.at[both, every, part], pair_tile.at[both, every, part], pair
+        return remote(src, dst, g_send.at[kind], g_recv.at[chunk, (0, 1, 2, 2, 3)[kind]], to)
+
+    def g_wait_far(chunk):
+        whole = far_tile.at[both, every, rows(chunk)]
+        remote(whole, whole, g_send.at[2], g_recv.at[chunk, 2], right).wait_recv()
+
+    def g_drain():
+        for kind in range(5):
+            planes = low_half if kind in (2, 3) else every
+            whole = far_tile.at[both, planes]
+            remote(whole, whole, g_send.at[kind], g_recv.at[0, 0], right).wait_send()
+
+    def h_copy(side, e, chunk):
+        return remote(
+            high.at[e, every, padded(chunk)], halo.at[e, side, every, rows(chunk)],
+            h_send.at[e, side], h_recv.at[e, chunk], after if side == 0 else before,
+        )
+
+    def h_start(e, chunk):
         @pl.when(has_after)
         def _():
-            h_copy(0, slot, e, chunk).start()
+            h_copy(0, e, chunk).start()
 
         @pl.when(has_before)
         def _():
-            h_copy(1, slot, e, chunk).start()
-
-    def h_wait_recv(slot, e, chunk):
+            h_copy(1, e, chunk).start()
+
+    inside = jnp.logical_and(has_before, has_after)
+
+    def h_wait_recv(e, chunk):
+        @pl.when(inside)
+        def _():
+            whole = halo.at[e, both, every, rows(chunk)]
+            remote(whole, whole, h_send.at[e, 0], h_recv.at[e, chunk], right).wait_recv()
+
+        @pl.when(jnp.logical_not(inside))
+        def _():
+            one = halo.at[e, 0, every, rows(chunk)]
+            remote(one, one, h_send.at[e, 0], h_recv.at[e, chunk], right).wait_recv()
+
+    def h_drain(e, _):
+        whole = halo.at[e, 0]
+
+        @pl.when(has_after)
+        def _():
+            remote(whole, whole, h_send.at[e, 0], h_recv.at[e, 0], right).wait_send()
+
         @pl.when(has_before)
         def _():
-            h_copy(0, slot, e, chunk).wait_recv()
-
-        @pl.when(has_after)
-        def _():
-            h_copy(1, slot, e, chunk).wait_recv()
-
-    def h_wait_send(slot, e, chunk):
-        @pl.when(has_after)
-        def _():
-            h_copy(0, slot, e, chunk).wait_send()
-
-        @pl.when(has_before)
-        def _():
-            h_copy(1, slot, e, chunk).wait_send()
+            remote(whole, whole, h_send.at[e, 1], h_recv.at[e, 0], right).wait_send()
+
+        return 0
 
     def r_copy(kind, b, chunk):
         part = rows(chunk)
@@ -189,25 +213,36 @@
         elif kind == 2:
             src, dst, to = far_out.at[b, high_half, part], far_in.at[b, high_half, part], left
         elif kind == 3:
-            src, dst, to = right_out.at[b, every, part], from_left.at[b, every, part], right
+            src, dst, to = right_out.at[b, every, part], near_in.at[b, 0, every, part], right
         else:
-            src, dst, to = left_out.at[b, every, part], from_right.at[b, every, part], left
-        return pltpu.make_async_remote_copy(
-            src_ref=src, dst_ref=dst, send_sem=r_send.at[b, chunk, kind],
-            recv_sem=r_recv.at[b, chunk, kind], device_id=to, device_id_type=MESH,
-        )
-
-    def put_split(slot, chunk, group, value):
+            src, dst, to = left_out.at[b, every, part], near_in.at[b, 1, every, part], left
+        return remote(src, dst, r_send.at[kind], r_recv.at[b, chunk, (0, 1, 1, 2, 2)[kind]], to)
+
+    def r_wait_far(b, chunk):
+        whole = far_in.at[b, every, rows(chunk)]
+        remote(whole, whole, r_send.at[1], r_recv.at[b, chunk, 1], right).wait_recv()
+
+    def r_wait_near(b, chunk):
+        whole = near_in.at[b, both, every, rows(chunk)]
+        remote(whole, whole, r_send.at[3], r_recv.at[b, chunk, 2], right).wait_recv()
+
+    def r_drain():
+        for kind in range(5):
+            planes = low_half if kind in (1, 2) else every
+            whole = far_in.at[both, planes]
+            remote(whole, whole, r_send.at[kind], r_recv.at[0, 0, 0], right).wait_send()
+
+    def put_split(e, slot, chunk, group, value):
         top = value.astype(BF16)
-        high[slot, :, padded(chunk, group), :] = top
+        high[e, :, padded(chunk, group), :] = top
         low[slot, :, padded(chunk, group), :] = (value - top.astype(F32)).astype(BF16)
 
-    def matrix_part(slot, chunk):
+    def matrix_part(e, slot, chunk):
         window = pl.ds(pl.multiple_of(chunk * ROWS, ROWS), WINDOW)
         columns = jnp.concatenate(
             [
-                jnp.concatenate([ref[slot, plane, window, :] for plane in range(PLANES)], axis=1)
-                for ref in (high, low)
+                jnp.concatenate([ref[at_, plane, window, :] for plane in range(PLANES)], axis=1)
+                for ref, at_ in ((high, e), (low, slot))
             ],
             axis=0,
         )
@@ -215,7 +250,7 @@
         lines = jnp.concatenate(
             [
                 jnp.concatenate(
-                    [high[slot, plane, padded(chunk), :], low[slot, plane, padded(chunk), :]], axis=1
+                    [high[e, plane, padded(chunk), :], low[slot, plane, padded(chunk), :]], axis=1
                 )
                 for plane in range(PLANES)
             ],
@@ -269,15 +304,15 @@
             + slopes[2, :, part, :] * diffs[2]
         )
 
-    def take_tile(a, chunk):
-        for kind in (0, 1):
-            g_copy(kind, a, chunk).start()
-
-    def relay_tile(a, chunk):
-        g_copy(0, a, chunk).wait_recv()
-        g_copy(2, a, chunk).start()
-        g_copy(1, a, chunk).wait_recv()
-        g_copy(3, a, chunk).start()
+    def take_tiles(chunk):
+        g_copy(0, chunk).start()
+        g_copy(1, chunk).start()
+
+    def relay_tiles(chunk):
+        g_copy(0, chunk).wait_recv()
+        g_copy(2, chunk).start()
+        g_copy(1, chunk).wait_recv()
+        g_copy(3, chunk).start()
 
     def chosen(a, part, flags):
         total = own_tile[a, :, part, :].astype(F32) * flags[0]
@@ -285,27 +320,26 @@
             total = total + ref[a, :, part, :].astype(F32) * one
         return total
 
-    def pair_tile_send(a, chunk):
-        g_copy(2, a, chunk).wait_recv()
-        g_copy(3, a, chunk).wait_recv()
-        for group in range(groups):
-            part = rows(chunk, group)
-            pair_out[a, :, part, :] = chosen(a, part, theirs_is).astype(BF16)
-        g_copy(4, a, chunk).start()
+    def pair_tiles(chunk):
+        g_wait_far(chunk)
+        for group in range(groups):
+            part = rows(chunk, group)
+            for a in (DEN, VEL):
+                pair_out[a, :, part, :] = chosen(a, part, theirs_is).astype(BF16)
+        g_copy(4, chunk).start()
 
     def finish_density(chunk):
-        g_copy(4, DEN, chunk).wait_recv()
+        g_copy(4, chunk).wait_recv()
         for group in range(groups):
             part = rows(chunk, group)
             value = chosen(DEN, part, mine_is) + pair_tile[DEN, :, part, :].astype(F32) * mine_pair
             density[:, part, :] = value
             logs = jnp.log(value)
             log_den[:, part, :] = logs
-            put_split(2, chunk, group, logs)
-        h_start(2, LOG, chunk)
+            put_split(LOG, 2, chunk, group, logs)
+        h_start(LOG, chunk)
 
     def finish_velocity(chunk):
-        g_copy(4, VEL, chunk).wait_recv()
         for group in range(groups):
             part = rows(chunk, group)
             velocity[:, part, :] = (
@@ -313,8 +347,8 @@
             )
 
     def make_slopes(chunk):
-        h_wait_recv(2, LOG, chunk)
-        matrix_part(2, chunk)
+        h_wait_recv(LOG, chunk)
+        matrix_part(LOG, 2, chunk)
         for group in range(groups):
             part = rows(chunk, group)
             _, diffs = vector_part(log_den[:, part, :], LOG, chunk, group, False)
@@ -323,12 +357,8 @@
 
     def forward(chunk, n):
         now, other = lax.rem(n, 2), lax.rem(n + 1, 2)
-        h_wait_recv(now, n, chunk)
-        matrix_part(now, chunk)
-
-        @pl.when(n > 0)
-        def _():
-            h_wait_send(other, n - 1, chunk)
+        h_wait_recv(n, chunk)
+        matrix_part(n, now, chunk)
 
         last = n == ITERS - 1
         for group in range(groups):
@@ -345,15 +375,14 @@
             source[n, :, part, :] = misfit
             following = jnp.where(last, adj[0, :, part, :] + misfit, moved)
             field[other, :, part, :] = following
-            put_split(other, chunk, group, following)
-        h_start(other, n + 1, chunk)
+            put_split(n + 1, other, chunk, group, following)
+        h_start(n + 1, chunk)
 
     def backward(chunk, n):
         now, other = lax.rem(n, 2), lax.rem(n + 1, 2)
         k = n - ITERS
-        h_wait_recv(now, n, chunk)
-        matrix_part(now, chunk)
-        h_wait_send(other, n - 1, chunk)
+        h_wait_recv(n, chunk)
+        matrix_part(n, now, chunk)
         for group in range(groups):
             part = rows(chunk, group)
             own = field[now, :, part, :]
@@ -364,7 +393,7 @@
             adj[other, :, part, :] = moved
             following = moved + source[2 - k, :, part, :]
             field[other, :, part, :] = following
-            put_split(other, chunk, group, following)
+            put_split(n + 1, other, chunk, group, following)
             total = sum_vel[:, part, :] + own * kept_l[3 - k, :, part, :]
             sum_vel[:, part, :] = total
             sum_den[:, part, :] += (
@@ -378,7 +407,7 @@
                 whole = total + following * kept_l[0, :, part, :]
                 shot_out[VEL, :, part, :] = (2.0 * SPEED * vel * whole).astype(BF16)
 
-        h_start(other, n + 1, chunk)
+        h_start(n + 1, chunk)
 
         @pl.when(k == 2)
         def _():
@@ -386,8 +415,8 @@
 
     def backward_last(chunk):
         n = 2 * ITERS - 1
-        h_wait_recv(n % 2, n, chunk)
-        matrix_part(n % 2, chunk)
+        h_wait_recv(n, chunk)
+        matrix_part(n, n % 2, chunk)
         for group in range(groups):
             part = rows(chunk, group)
             own = field[n % 2, :, part, :]
@@ -418,8 +447,7 @@
         r_copy(2, b, chunk).start()
 
     def reduce_near(b, chunk):
-        r_copy(1, b, chunk).wait_recv()
-        r_copy(2, b, chunk).wait_recv()
+        r_wait_far(b, chunk)
         for group in range(groups):
             part = rows(chunk, group)
             arrived = far_in[b, :, part, :].astype(F32)
@@ -433,29 +461,18 @@
         r_copy(4, b, chunk).start()
 
     def reduce_end(b, chunk):
-        r_copy(3, b, chunk).wait_recv()
-        r_copy(4, b, chunk).wait_recv()
+        r_wait_near(b, chunk)
         out = grad_vel if b == VEL else grad_den
         for group in range(groups):
             part = rows(chunk, group)
             out[0, :, part, :] = (
                 for_step(b, part, 0)
-                + from_left[b, :, part, :].astype(F32)
-                + from_right[b, :, part, :].astype(F32)
+                + near_in[b, 0, :, part, :].astype(F32)
+                + near_in[b, 1, :, part, :].astype(F32)
             )
 
-    loads[0].wait()
-    loads[1].wait()
-
-    barrier_count = 3 + has_after.astype(jnp.int32) + has_before.astype(jnp.int32)
-    pl.semaphore_wait(barrier, barrier_count)
-
-    for chunk in range(2):
-        take_tile(DEN, chunk)
-        take_tile(VEL, chunk)
-
-    edge = jnp.zeros((3, PLANES, PAD, LANES), BF16)
     for ref in (high, low):
+        edge = jnp.zeros((ref.shape[0], PLANES, PAD, LANES), BF16)
         ref[:, :, 0:PAD, :] = edge
         ref[:, :, PAD + chunks * ROWS :, :] = edge
 
@@ -473,8 +490,7 @@
 
     def first_field(chunk, _):
         for group in range(groups):
-            put_split(0, chunk, group, field[0, :, rows(chunk, group), :])
-        h_start(0, 0, chunk)
+            put_split(0, 0, chunk, group, field[0, :, rows(chunk, group), :])
         return 0
 
     lax.fori_loop(0, chunks, first_field, 0)
@@ -513,6 +529,20 @@
     lax.fori_loop(0, PLANES, clear_sums, 0)
     receiver_lanes()
 
+    loads[0].wait()
+    loads[1].wait()
+    barrier_count = 3 + has_after.astype(jnp.int32) + has_before.astype(jnp.int32)
+    pl.semaphore_wait(barrier, barrier_count)
+
+    for chunk in range(2):
+        take_tiles(chunk)
+
+    def first_halo(chunk, _):
+        h_start(0, chunk)
+        return 0
+
+    lax.fori_loop(0, chunks, first_halo, 0)
+
     for load in loads[3:]:
         load.wait()
 
@@ -528,25 +558,13 @@
             receivers_of_plane(2 * pair_index)
             receivers_of_plane(2 * pair_index + 1)
 
-        def next_tiles(chunk):
-            take_tile(DEN, chunk)
-            take_tile(VEL, chunk)
-
-        def relays(chunk):
-            relay_tile(DEN, chunk)
-            relay_tile(VEL, chunk)
-
-        def pairs(chunk):
-            pair_tile_send(DEN, chunk)
-            pair_tile_send(VEL, chunk)
-
         def finish(chunk):
             finish_density(chunk)
             finish_velocity(chunk)
 
-        at(t, relays)
-        at(t + 2, next_tiles)
-        at(t - 1, pairs)
+        at(t, relay_tiles)
+        at(t + 2, take_tiles)
+        at(t - 1, pair_tiles)
         at(t - 2, finish)
         pl.when(t < 2)(lambda: plane_pair(t))
         wave = t - first_wave
@@ -573,17 +591,9 @@
 
     lax.fori_loop(0, ticks, tick, 0)
 
-    def drain(chunk, _):
-        for a in range(2):
-            for kind in range(5):
-                g_copy(kind, a, chunk).wait_send()
-                r_copy(kind, a, chunk).wait_send()
-        h_wait_send(0, 6, chunk)
-        h_wait_send(1, 7, chunk)
-        h_wait_send(2, LOG, chunk)
-        return 0
-
-    lax.fori_loop(0, chunks, drain, 0)
+    g_drain()
+    lax.fori_loop(0, 9, h_drain, 0)
+    r_drain()
 
 
 def body(vel_model, den_model, cover, receivers, observed, p_now, p_before, q_now, q_before):
@@ -598,7 +608,7 @@
     return pl.pallas_call(
         functools.partial(kernel, n_shot, n_sub, chunks),
         name="window",
-        out_shape=(out, out),
+        out_shape=(pltpu.VMEM(out.shape, F32), pltpu.VMEM(out.shape, F32)),
         in_specs=[pl.BlockSpec(memory_space=pltpu.SMEM)] + [vmem] * 4 + [anywhere] * 6,
         out_specs=(vmem, vmem),
         scratch_shapes=[
@@ -607,7 +617,7 @@
             pltpu.VMEM(tile, F32),
             pltpu.VMEM(tile, F32),
             pltpu.VMEM((3, *tile), F32),
-            pltpu.VMEM((3, *tall), BF16),
+            pltpu.VMEM((9, *tall), BF16),
             pltpu.VMEM((3, *tall), BF16),
             pltpu.VMEM((9, 2, *tile), BF16),
             pltpu.VMEM((2, *tile), F32),
@@ -620,16 +630,17 @@
             pltpu.VMEM(tile, F32),
             pltpu.VMEM((2 * ROWS, PLANES * LANES), F32),
             pltpu.VMEM((PLANES * ROWS, 2 * LANES), F32),
-            *[pltpu.VMEM((2, *tile), BF16) for _ in range(8)],
+            *[pltpu.VMEM((2, *tile), BF16) for _ in range(6)],
+            pltpu.VMEM((2, 2, *tile), BF16),
             pltpu.VMEM((LANES, receivers.shape[1]), BF16),
             pltpu.VMEM((ITERS, LANES, 2 * receivers.shape[1]), BF16),
             pltpu.SemaphoreType.DMA((6,)),
-            pltpu.SemaphoreType.DMA((2, chunks, 5)),
-            pltpu.SemaphoreType.DMA((2, chunks, 5)),
-            pltpu.SemaphoreType.DMA((9, chunks, 2)),
-            pltpu.SemaphoreType.DMA((9, chunks, 2)),
-            pltpu.SemaphoreType.DMA((2, chunks, 5)),
-            pltpu.SemaphoreType.DMA((2, chunks, 5)),
+            pltpu.SemaphoreType.DMA((5,)),
+            pltpu.SemaphoreType.DMA((chunks, 4)),
+            pltpu.SemaphoreType.DMA((9, 2)),
+            pltpu.SemaphoreType.DMA((9, chunks)),
+            pltpu.SemaphoreType.DMA((5,)),
+            pltpu.SemaphoreType.DMA((2, chunks, 3)),
         ],
         compiler_params=pltpu.CompilerParams(
             collective_id=0, has_side_effects=True, vmem_limit_bytes=60 * 1024 * 1024

time: 102 us -> 97.9 us (0.960)
  Pallas kernels: 98 us -> 95.3 us
  local copies, waits for them, and re-layouts: 2.87 us -> 1.67 us
    pallas_call x1, Pallas kernels: 98 us -> 95.3 us  [body(): pl.pallas_call(functools.partial(kernel, n_shot, n_sub, chunks), name='wi...]
    unnamed x4 -> x2, local copies, waits for them, and re-layouts: 2.87 us -> 1.67 us
where the time goes in v3:
time: 97.9 us; the launch traced here: 97.7 us
  Pallas kernels  95.3 us (97%)
  local copies, waits for them, and re-layouts  1.67 us (2%)
    pallas_call x1, Pallas kernels, body(): pl.pallas_call(functools.partial(kernel, n_shot, n_sub, chunks), name='wi...  95.3 us

profile of v3, /device:TPU:232, one launch (start us, length us, event | category | flops | bytes accessed | tf_op | source)
XLA Modules:
  0.0 97.7 jit_solution(1221341003932759258)
XLA Ops:
  0.6 95.3 %window.1 = (f32[1,4,320,128]{3,2,1,0:T(8,128)S(1)}, f32[1,4,320,128]{3,2,1,0:T(8,128)S(1)}) custom-call(s32[8,32]{1,0:T(8,128)} %cover.1, s32[1,512]{1,0:T(1,128)} %receivers.1, f32[1,4,512]{2,1,0:T(4,128)} %observed.1, bf16[128,192]{1,0:T(8,128)(2,1)} %constant.4.clone.taps_y, bf16[256,256]{1,0:T(8,128)(2,1)} %constant.5.clone.taps_z, ...), custom_call_target="tpu_custom_call" | custom-call | tf_op jit(solution)/shard_map/window/pallas_call | solution.py:608
  96.0 0.8 copy.15
  96.8 0.8 copy.16

commit v4 on v3

--- a/solution.py
+++ b/solution.py
@@ -28,6 +28,8 @@
 SUB = 16
 LOG = 8
 DEN, VEL = 0, 1
+TILES_DIRECT = 0
+SUMS_DIRECT = (1, 0)
 
 
 def band_y():
@@ -71,6 +73,7 @@
     c = lax.axis_index("sub")
     right = (lax.rem(s + 2, n_shot), c)
     left = (lax.rem(s + n_shot - 2, n_shot), c)
+    far = (lax.rem(s + 4, n_shot), c)
     y_hi = lax.rem(s, 2)
     pair = (s + 1 - 2 * y_hi, c)
     after = (s, c + 1)
@@ -90,7 +93,7 @@
         load.start()
 
     barrier = pltpu.get_barrier_semaphore()
-    for other in (right, left, pair):
+    for other in (right, left, far, pair):
         pl.semaphore_signal(barrier, 1, device_id=other, device_id_type=MESH)
 
     @pl.when(has_after)
@@ -129,6 +132,8 @@
     every = pl.ds(0, PLANES)
 
     both = pl.ds(0, 2)
+    tiles_relayed = chunks - TILES_DIRECT
+    sums_relayed = (chunks - SUMS_DIRECT[DEN], chunks - SUMS_DIRECT[VEL])
 
     def remote(src, dst, send, recv, to):
         return pltpu.make_async_remote_copy(
@@ -149,19 +154,23 @@
             src, dst, to = (
                 right_tile.at[both, high_half, part], far_tile.at[both, high_half, part], left
             )
+        elif kind == 4:
+            src, dst, to = pair_out.at[both, every, part], pair_tile.at[both, every, part], pair
         else:
-            src, dst, to = pair_out.at[both, every, part], pair_tile.at[both, every, part], pair
-        return remote(src, dst, g_send.at[kind], g_recv.at[chunk, (0, 1, 2, 2, 3)[kind]], to)
+            src, dst, to = own_tile.at[both, every, part], far_tile.at[both, every, part], far
+        return remote(src, dst, g_send.at[kind], g_recv.at[chunk, (0, 1, 2, 2, 3, 2)[kind]], to)
 
     def g_wait_far(chunk):
         whole = far_tile.at[both, every, rows(chunk)]
         remote(whole, whole, g_send.at[2], g_recv.at[chunk, 2], right).wait_recv()
 
     def g_drain():
-        for kind in range(5):
+        for kind in range(6):
             planes = low_half if kind in (2, 3) else every
-            whole = far_tile.at[both, planes]
-            remote(whole, whole, g_send.at[kind], g_recv.at[0, 0], right).wait_send()
+            sent = {2: tiles_relayed, 3: tiles_relayed, 5: chunks - tiles_relayed}.get(kind, chunks)
+            if sent:
+                whole = far_tile.at[both, planes, pl.ds(0, sent * ROWS)]
+                remote(whole, whole, g_send.at[kind], g_recv.at[0, 0], right).wait_send()
 
     def h_copy(side, e, chunk):
         return remote(
@@ -214,23 +223,31 @@
             src, dst, to = far_out.at[b, high_half, part], far_in.at[b, high_half, part], left
         elif kind == 3:
             src, dst, to = right_out.at[b, every, part], near_in.at[b, 0, every, part], right
+        elif kind == 4:
+            src, dst, to = left_out.at[b, every, part], near_in.at[b, 1, every, part], left
         else:
-            src, dst, to = left_out.at[b, every, part], near_in.at[b, 1, every, part], left
-        return remote(src, dst, r_send.at[kind], r_recv.at[b, chunk, (0, 1, 1, 2, 2)[kind]], to)
+            src, dst, to = far_out.at[b, every, part], far_in.at[b, every, part], far
+        return remote(
+            src, dst, r_send.at[b, kind], r_recv.at[b, chunk, (0, 1, 1, 2, 2, 1)[kind]], to
+        )
 
     def r_wait_far(b, chunk):
         whole = far_in.at[b, every, rows(chunk)]
-        remote(whole, whole, r_send.at[1], r_recv.at[b, chunk, 1], right).wait_recv()
+        remote(whole, whole, r_send.at[b, 1], r_recv.at[b, chunk, 1], right).wait_recv()
 
     def r_wait_near(b, chunk):
         whole = near_in.at[b, both, every, rows(chunk)]
-        remote(whole, whole, r_send.at[3], r_recv.at[b, chunk, 2], right).wait_recv()
+        remote(whole, whole, r_send.at[b, 3], r_recv.at[b, chunk, 2], right).wait_recv()
 
     def r_drain():
-        for kind in range(5):
-            planes = low_half if kind in (1, 2) else every
-            whole = far_in.at[both, planes]
-            remote(whole, whole, r_send.at[kind], r_recv.at[0, 0, 0], right).wait_send()
+        for b in (DEN, VEL):
+            for kind in range(6):
+                planes = low_half if kind in (1, 2) else every
+                relayed = sums_relayed[b]
+                sent = {1: relayed, 2: relayed, 5: chunks - relayed}.get(kind, chunks)
+                if sent:
+                    whole = far_in.at[b, planes, pl.ds(0, sent * ROWS)]
+                    remote(whole, whole, r_send.at[b, kind], r_recv.at[0, 0, 0], right).wait_send()
 
     def put_split(e, slot, chunk, group, value):
         top = value.astype(BF16)
@@ -307,12 +324,13 @@
     def take_tiles(chunk):
         g_copy(0, chunk).start()
         g_copy(1, chunk).start()
+        pl.when(chunk >= tiles_relayed)(lambda: g_copy(5, chunk).start())
 
     def relay_tiles(chunk):
         g_copy(0, chunk).wait_recv()
-        g_copy(2, chunk).start()
+        pl.when(chunk < tiles_relayed)(lambda: g_copy(2, chunk).start())
         g_copy(1, chunk).wait_recv()
-        g_copy(3, chunk).start()
+        pl.when(chunk < tiles_relayed)(lambda: g_copy(3, chunk).start())
 
     def chosen(a, part, flags):
         total = own_tile[a, :, part, :].astype(F32) * flags[0]
@@ -440,25 +458,41 @@
 
     def reduce_far(b, chunk):
         r_copy(0, b, chunk).wait_recv()
+        straight = chunk >= sums_relayed[b]
         for group in range(groups):
             part = rows(chunk, group)
             far_out[b, :, part, :] = for_step(b, part, 3).astype(BF16)
-        r_copy(1, b, chunk).start()
-        r_copy(2, b, chunk).start()
+
+        @pl.when(straight)
+        def _():
+            r_copy(5, b, chunk).start()
+            for group in range(groups):
+                part = rows(chunk, group)
+                right_out[b, :, part, :] = for_step(b, part, 2).astype(BF16)
+                left_out[b, :, part, :] = for_step(b, part, 1).astype(BF16)
+            r_copy(3, b, chunk).start()
+            r_copy(4, b, chunk).start()
+
+        @pl.when(jnp.logical_not(straight))
+        def _():
+            r_copy(1, b, chunk).start()
+            r_copy(2, b, chunk).start()
 
     def reduce_near(b, chunk):
-        r_wait_far(b, chunk)
-        for group in range(groups):
-            part = rows(chunk, group)
-            arrived = far_in[b, :, part, :].astype(F32)
-            to_right = for_step(b, part, 2)
-            to_left = for_step(b, part, 1)
-            right_out[b, 0:2, part, :] = (to_right[0:2] + arrived[0:2]).astype(BF16)
-            right_out[b, 2:4, part, :] = to_right[2:4].astype(BF16)
-            left_out[b, 0:2, part, :] = to_left[0:2].astype(BF16)
-            left_out[b, 2:4, part, :] = (to_left[2:4] + arrived[2:4]).astype(BF16)
-        r_copy(3, b, chunk).start()
-        r_copy(4, b, chunk).start()
+        @pl.when(chunk < sums_relayed[b])
+        def _():
+            r_wait_far(b, chunk)
+            for group in range(groups):
+                part = rows(chunk, group)
+                arrived = far_in[b, :, part, :].astype(F32)
+                to_right = for_step(b, part, 2)
+                to_left = for_step(b, part, 1)
+                right_out[b, 0:2, part, :] = (to_right[0:2] + arrived[0:2]).astype(BF16)
+                right_out[b, 2:4, part, :] = to_right[2:4].astype(BF16)
+                left_out[b, 0:2, part, :] = to_left[0:2].astype(BF16)
+                left_out[b, 2:4, part, :] = (to_left[2:4] + arrived[2:4]).astype(BF16)
+            r_copy(3, b, chunk).start()
+            r_copy(4, b, chunk).start()
 
     def reduce_end(b, chunk):
         r_wait_near(b, chunk)
@@ -470,6 +504,13 @@
                 + near_in[b, 0, :, part, :].astype(F32)
                 + near_in[b, 1, :, part, :].astype(F32)
             )
+
+        @pl.when(chunk >= sums_relayed[b])
+        def _():
+            r_wait_far(b, chunk)
+            for group in range(groups):
+                part = rows(chunk, group)
+                out[0, :, part, :] += far_in[b, :, part, :].astype(F32)
 
     for ref in (high, low):
         edge = jnp.zeros((ref.shape[0], PLANES, PAD, LANES), BF16)
@@ -531,7 +572,7 @@
 
     loads[0].wait()
     loads[1].wait()
-    barrier_count = 3 + has_after.astype(jnp.int32) + has_before.astype(jnp.int32)
+    barrier_count = 4 + has_after.astype(jnp.int32) + has_before.astype(jnp.int32)
     pl.semaphore_wait(barrier, barrier_count)
 
     for chunk in range(2):
@@ -635,11 +676,11 @@
             pltpu.VMEM((LANES, receivers.shape[1]), BF16),
             pltpu.VMEM((ITERS, LANES, 2 * receivers.shape[1]), BF16),
             pltpu.SemaphoreType.DMA((6,)),
-            pltpu.SemaphoreType.DMA((5,)),
+            pltpu.SemaphoreType.DMA((6,)),
             pltpu.SemaphoreType.DMA((chunks, 4)),
             pltpu.SemaphoreType.DMA((9, 2)),
             pltpu.SemaphoreType.DMA((9, chunks)),
-            pltpu.SemaphoreType.DMA((5,)),
+            pltpu.SemaphoreType.DMA((2, 6)),
             pltpu.SemaphoreType.DMA((2, chunks, 3)),
         ],
         compiler_params=pltpu.CompilerParams(

time: 97.9 us -> 95.8 us (0.979)
  Pallas kernels: 95.3 us -> 92.9 us
    pallas_call x1, Pallas kernels: 95.3 us -> 92.9 us  [body(): pl.pallas_call(functools.partial(kernel, n_shot, n_sub, chunks), name='wi...]
where the time goes in v4:
time: 95.8 us; the launch traced here: 95.2 us
  Pallas kernels  92.9 us (97%)
  local copies, waits for them, and re-layouts  1.67 us (2%)
    pallas_call x1, Pallas kernels, body(): pl.pallas_call(functools.partial(kernel, n_shot, n_sub, chunks), name='wi...  92.9 us

profile of v4, /device:TPU:232, one launch (start us, length us, event | category | flops | bytes accessed | tf_op | source)
XLA Modules:
  0.0 95.2 jit_solution(896382096469995745)
XLA Ops:
  0.6 92.9 %window.1 = (f32[1,4,320,128]{3,2,1,0:T(8,128)S(1)}, f32[1,4,320,128]{3,2,1,0:T(8,128)S(1)}) custom-call(s32[8,32]{1,0:T(8,128)} %cover.1, s32[1,512]{1,0:T(1,128)} %receivers.1, f32[1,4,512]{2,1,0:T(4,128)} %observed.1, bf16[128,192]{1,0:T(8,128)(2,1)} %constant.4.clone.taps_y, bf16[256,256]{1,0:T(8,128)(2,1)} %constant.5.clone.taps_z, ...), custom_call_target="tpu_custom_call" | custom-call | tf_op jit(solution)/shard_map/window/pallas_call | solution.py:649
  93.6 0.8 copy.15
  94.4 0.8 copy.16

commit v5 on v4

--- a/solution.py
+++ b/solution.py
@@ -450,6 +450,14 @@
             ).astype(BF16)
         r_copy(0, DEN, chunk).start()
 
+    def whole_flag(one):
+        return jnp.full((1, SUB, LANES), one, F32).astype(BF16)
+
+    def sent_step(b, part, which):
+        return shot_out[b, :, part, :] * whole_flag(mine_is[which]) + shot_pair[
+            b, :, part, :
+        ] * whole_flag(theirs_is[which])
+
     def for_step(b, part, which):
         return (
             shot_out[b, :, part, :].astype(F32) * mine_is[which]
@@ -461,15 +469,15 @@
         straight = chunk >= sums_relayed[b]
         for group in range(groups):
             part = rows(chunk, group)
-            far_out[b, :, part, :] = for_step(b, part, 3).astype(BF16)
+            far_out[b, :, part, :] = sent_step(b, part, 3)
 
         @pl.when(straight)
         def _():
             r_copy(5, b, chunk).start()
             for group in range(groups):
                 part = rows(chunk, group)
-                right_out[b, :, part, :] = for_step(b, part, 2).astype(BF16)
-                left_out[b, :, part, :] = for_step(b, part, 1).astype(BF16)
+                right_out[b, :, part, :] = sent_step(b, part, 2)
+                left_out[b, :, part, :] = sent_step(b, part, 1)
             r_copy(3, b, chunk).start()
             r_copy(4, b, chunk).start()
 
@@ -484,13 +492,13 @@
             r_wait_far(b, chunk)
             for group in range(groups):
                 part = rows(chunk, group)
-                arrived = far_in[b, :, part, :].astype(F32)
-                to_right = for_step(b, part, 2)
-                to_left = for_step(b, part, 1)
-                right_out[b, 0:2, part, :] = (to_right[0:2] + arrived[0:2]).astype(BF16)
-                right_out[b, 2:4, part, :] = to_right[2:4].astype(BF16)
-                left_out[b, 0:2, part, :] = to_left[0:2].astype(BF16)
-                left_out[b, 2:4, part, :] = (to_left[2:4] + arrived[2:4]).astype(BF16)
+                arrived = far_in[b, :, part, :]
+                to_right = sent_step(b, part, 2)
+                to_left = sent_step(b, part, 1)
+                right_out[b, 0:2, part, :] = to_right[0:2] + arrived[0:2]
+                right_out[b, 2:4, part, :] = to_right[2:4]
+                left_out[b, 0:2, part, :] = to_left[0:2]
+                left_out[b, 2:4, part, :] = to_left[2:4] + arrived[2:4]
             r_copy(3, b, chunk).start()
             r_copy(4, b, chunk).start()
 
@@ -626,14 +634,17 @@
         lax.fori_loop(
             jnp.maximum(wave - (chunks - 1), 0), jnp.minimum(wave + 1, 2 * ITERS), process, 0
         )
+        @pl.when(wave == n_waves)
+        def _():
+            g_drain()
+            lax.fori_loop(0, 9, h_drain, 0)
+
         reduce_lag(VEL, 6)
         reduce_lag(DEN, 7)
         return 0
 
     lax.fori_loop(0, ticks, tick, 0)
 
-    g_drain()
-    lax.fori_loop(0, 9, h_drain, 0)
     r_drain()
 
 

time: 95.8 us -> 95.7 us (level)
  no operation moved by 1% of the time
where the time goes in v5:
time: 95.7 us; the launch traced here: 95.2 us
  Pallas kernels  92.9 us (97%)
  local copies, waits for them, and re-layouts  1.67 us (2%)
    pallas_call x1, Pallas kernels, body(): pl.pallas_call(functools.partial(kernel, n_shot, n_sub, chunks), name='wi...  92.9 us

profile of v5, /device:TPU:232, one launch (start us, length us, event | category | flops | bytes accessed | tf_op | source)
XLA Modules:
  0.0 95.2 jit_solution(13717616565278776834)
XLA Ops:
  0.6 92.9 %window.1 = (f32[1,4,320,128]{3,2,1,0:T(8,128)S(1)}, f32[1,4,320,128]{3,2,1,0:T(8,128)S(1)}) custom-call(s32[8,32]{1,0:T(8,128)} %cover.1, s32[1,512]{1,0:T(1,128)} %receivers.1, f32[1,4,512]{2,1,0:T(4,128)} %observed.1, bf16[128,192]{1,0:T(8,128)(2,1)} %constant.4.clone.taps_y, bf16[256,256]{1,0:T(8,128)(2,1)} %constant.5.clone.taps_z, ...), custom_call_target="tpu_custom_call" | custom-call | tf_op jit(solution)/shard_map/window/pallas_call | solution.py:660
  93.5 0.8 copy.15
  94.3 0.8 copy.16
